TPU v7x, 32 devices: a whole 2x2x4 slice. The times are simulated.
32 devices in a mesh: seq: 16 (over z, x, core), head: 2 (over y).
Axes of the slice: x: 2, y: 2, z: 4, core: 2. Of those that a mesh axis runs over, the one named last changes fastest.
Arguments:
- queries: bfloat16 [11264, 4096], P(('seq', 'head')), may hold values from -64 to 64
- database_rows: bfloat16 [128, 64, 896], P('seq', 'head'), may hold values from -6 to 6
- w_encoder: bfloat16 [896, 896], P('seq'), may hold values from -0.1875 to 0.1875
- w_key: bfloat16 [896, 4096], P(None, 'head'), may hold values from -0.1875 to 0.1875
- w_value: bfloat16 [896, 4096], P(None, 'head'), may hold values from -0.1875 to 0.1875
- neighbour_ids: int32 [176, 2], replicated, may hold values from 0 to 127, as said below
Outputs:
- attended: bfloat16 [11264, 4096], P(('seq', 'head'))
Inputs may be any that keep to these rules, and one draw needn't show every extreme that they name: `neighbour_ids`: among the 22 neighbours of the spans of one sequence shard (rows s * 11 onward), at most 2 are entries of any one database shard, and in every shard some database shard holds exactly 2 of them. The same entry may appear more than once.
All inputs are finite; a program needn't handle non-finite values.
Results may differ from a plain program's by a relative error of at most 0.012.
The roundings to bfloat16 on the way count: a program that leaves them out, or rounds other values in their place, can miss the bound.
Values may be sent and summed in bfloat16 or wider, within the bound.
No kernel may reach another device: no remote copies, remote signals or barrier semaphores. Data moves between devices by JAX's collectives and lax.ppermute only.
A program may use at most 64 MiB of HBM per device.

v0:
```python
import jax
import jax.numpy as jnp
from jax import lax
from jax.sharding import PartitionSpec as P

HEAD_DIM = 128
SPAN = 64
NBR_LEN = 64
K_NBR = 2
DB_DEV = 8


def encode_rows(raw_rows, w_encoder):
    values_in = raw_rows.astype(jnp.float32)
    mean_square = jnp.mean(values_in * values_in, axis=-1, keepdims=True)
    normed = (values_in * lax.rsqrt(mean_square + 1e-06)).astype(jnp.bfloat16)
    flat_normed = normed.reshape(-1, normed.shape[-1])
    summed = jnp.dot(
        flat_normed,
        lax.all_gather(w_encoder, "seq", axis=0, tiled=True),
        preferred_element_type=jnp.float32,
    )
    return (values_in + jax.nn.silu(summed.reshape(values_in.shape))).astype(jnp.bfloat16)


def attend_spans(query_rows, keys, values):
    heads_here = query_rows.shape[1] // HEAD_DIM
    span_count = query_rows.shape[0] // SPAN
    query_block = query_rows.reshape(span_count, SPAN, heads_here, HEAD_DIM)
    key_block = keys.reshape(span_count, K_NBR * NBR_LEN, heads_here, HEAD_DIM)
    value_block = values.reshape(span_count, K_NBR * NBR_LEN, heads_here, HEAD_DIM)
    scores = jnp.einsum(
        "cqhd,ckhd->chqk", query_block, key_block, preferred_element_type=jnp.float32
    ) * HEAD_DIM ** (-0.5)
    highest = jnp.max(scores, axis=-1, keepdims=True)
    weights = jnp.exp(scores - highest)
    probs = (weights / jnp.sum(weights, axis=-1, keepdims=True)).astype(jnp.bfloat16)
    mixed = jnp.einsum("chqk,ckhd->cqhd", probs, value_block, preferred_element_type=jnp.float32)
    return mixed.astype(jnp.bfloat16).reshape(query_rows.shape)


def per_device(queries, database_rows, w_encoder, w_key, w_value, neighbour_ids):
    seq_count = lax.axis_size("seq")
    seq_index = lax.axis_index("seq")
    head_rows = lax.all_to_all(queries, "head", split_axis=1, concat_axis=0, tiled=True)
    encoded = encode_rows(database_rows, w_encoder)
    by_shard = neighbour_ids.reshape(seq_count, -1)
    cited_count = by_shard.shape[1]
    cap_count = max(2, (cited_count + seq_count - 1) // seq_count)
    cited_ids = lax.dynamic_index_in_dim(by_shard, seq_index, 0, keepdims=False)
    owners = by_shard // DB_DEV
    local_entry = by_shard % DB_DEV
    position = jnp.arange(cited_count, dtype=jnp.int32)
    same_owner = (owners[:, :, None] == owners[:, None, :]) & (
        position[None, None, :] < position[None, :, None]
    )
    earlier = jnp.sum(same_owner.astype(jnp.int32), axis=2)
    owned_here = owners == seq_index
    slot_index = jnp.arange(cap_count, dtype=jnp.int32)
    matches = owned_here[:, None, :] & (earlier[:, None, :] == slot_index[None, :, None])
    source_entry = jnp.sum(jnp.where(matches, local_entry[:, None, :], 0), axis=2)
    slot_filled = jnp.any(matches, axis=2)
    outgoing = jnp.where(
        slot_filled[:, :, None, None], encoded[source_entry], jnp.zeros((), jnp.bfloat16)
    )
    arrived = lax.all_to_all(outgoing, "seq", split_axis=0, concat_axis=0, tiled=True)
    cited_owner = cited_ids // DB_DEV
    cited_slot = lax.dynamic_index_in_dim(earlier, seq_index, 0, keepdims=False)
    flat_arrived = arrived.reshape(-1, arrived.shape[2], arrived.shape[3])
    neighbours = flat_arrived[cited_owner * cap_count + cited_slot]
    full_rows = lax.all_gather(neighbours, "head", axis=1, tiled=True)
    flat_rows = full_rows.reshape(-1, full_rows.shape[2])
    keys = jnp.dot(flat_rows, w_key, preferred_element_type=jnp.float32).astype(jnp.bfloat16)
    values = jnp.dot(flat_rows, w_value, preferred_element_type=jnp.float32).astype(jnp.bfloat16)
    mixed = attend_spans(head_rows, keys, values)
    return lax.all_to_all(mixed, "head", split_axis=0, concat_axis=1, tiled=True)


def solution(mesh):
    placed = (
        P(("seq", "head"), None),
        P("seq", "head", None),
        P("seq", None),
        P(None, "head"),
        P(None, "head"),
        P(),
    )
    return jax.shard_map(
        per_device, mesh=mesh, in_specs=placed, out_specs=P(("seq", "head"), None), check_vma=False
    )
```

profile of v0, /device:TPU:3, one launch (start us, length us, event | category | flops | bytes accessed | tf_op | source)
XLA Modules:
  0.0 272.9 jit_solution(3112015279693485701)
XLA Ops:
  6.5 0.0 all-gather.4.cloned.1.call-start
  6.5 0.7 all-gather.4.cloned.1.call-update
  7.3 0.8 copy.36
  8.1 0.1 reshape.250
  8.2 0.1 copy.37
  8.3 0.5 convert_reduce_fusion
  8.8 0.1 copy.38
  8.9 0.1 fusion.31
  9.0 0.1 copy.39
  9.1 0.1 select_reduce_fusion
  9.2 0.1 copy.40
  9.3 0.1 reshape.258
  9.4 1.2 fusion.19
  10.6 39.4 %all-gather.4.cloned.1.call-done = bf16[896,896]{1,0:T(8,128)(2,1)} async-done(((bf16[56,896]{1,0:T(8,128)(2,1)}), bf16[896,896]{1,0:T(8,128)(2,1)}) %all-gather.4.cloned.1.call-update) | async-done | bytes 1605648 | tf_op jit(solution)/shard_map/all_gather | solution.py:20
  50.1 2.4 fusion.21
  52.5 0.8 gather_fusion
  53.4 1.5 broadcast_select_fusion
  54.8 4.9 %all-to-all-start = ((bf16[16,2,32,896]{3,2,1,0:T(8,128)(2,1)}), bf16[16,2,32,896]{3,2,1,0:T(8,128)(2,1)S(1)}, u32[]{:S(2)}, u32[]{:S(2)}) async-start(bf16[16,2,32,896]{3,2,1,0:T(8,128)(2,1)} %broadcast_select_fusion), calls=%async_computation | async-start | bytes 3670016 | tf_op jit(solution)/shard_map/all_to_all | solution.py:66
  59.7 0.0 all-gather.6.cloned.1.call-start
  59.7 0.2 dynamic-slice_reduce_fusion
  60.0 38.0 %all-to-all-done = bf16[16,2,32,896]{3,2,1,0:T(8,128)(2,1)S(1)} async-done(((bf16[16,2,32,896]{3,2,1,0:T(8,128)(2,1)}), bf16[16,2,32,896]{3,2,1,0:T(8,128)(2,1)S(1)}, u32[]{:S(2)}, u32[]{:S(2)}) %all-to-all-start) | async-done | bytes 1835040 | tf_op jit(solution)/shard_map/all_to_all | solution.py:66
  98.0 1.8 gather_fusion.1
  99.8 0.0 all-gather.6.cloned.1.call-update
  99.8 2.0 copy.61
  101.8 60.5 %all_to_all.40 = bf16[352,2,2048]{2,0,1:T(8,128)(2,1)S(1)} all-to-all(bf16[352,2,2048]{2,0,1:T(8,128)(2,1)S(1)} %bitcast.79), channel_id=1, replica_groups=mesh['seq'=16,'head'=2] {'head'}, dimensions={1} | all-to-all | bytes 5767168 | tf_op jit(solution)/shard_map/all_to_all | solution.py:45
  162.3 0.9 copy.50
  163.2 2.3 all-gather.6.cloned.1.call-done
  165.5 8.6 %fusion.14 = bf16[176,8,16,128]{3,1,2,0:T(8,128)(2,1)S(1)} fusion(bf16[1408,896]{1,0:T(8,128)(2,1)} %bitcast.84, bf16[896,2048]{1,0:T(8,128)(2,1)} %param.9), kind=kOutput, calls=%fused_computation.21 | convolution fusion | flops 5170266112 | bytes 11960320 | tf_op jit(solution)/shard_map/dot_general | solution.py:73
  174.1 2.1 copy.49
  176.3 4.1 %fusion.5 = f32[11,16,128,64]{2,3,1,0:T(8,128)S(1)} fusion(bf16[11,128,16,128]{3,2,1,0:T(8,128)(2,1)S(1)} %bitcast.75, bf16[11,64,16,128]{3,2,1,0:T(8,128)(2,1)S(1)} %bitcast.76), kind=kOutput, calls=%fused_computation.11 | convolution fusion | flops 369098752 | bytes 14417920 | tf_op jit(solution)/shard_map/cqhd,ckhd->chqk/dot_general | solution.py:32
  180.3 0.0 copy-start
  180.3 0.0 copy-start.1
  180.3 0.0 copy-start.2
  180.4 3.0 %fusion.39 = f32[11,16,64]{2,1,0:T(8,128)S(1)} fusion(f32[11,16,128,64]{2,3,1,0:T(8,128)S(1)} %fusion.5), kind=kOutput, calls=%fused_computation.63 | output fusion | flops 5767295 | bytes 5812224 | tf_op jit(solution)/shard_map/sub | solution.py:36
  183.4 1.1 copy-done.1
  184.5 0.8 copy-done.2
  185.2 6.4 %fusion.13 = bf16[176,8,16,128]{3,1,2,0:T(8,128)(2,1)S(1)} fusion(bf16[1408,896]{1,0:T(8,128)(2,1)S(1)} %bitcast.85, bf16[896,2048]{1,0:T(8,128)(2,1)S(1)} %copy-done.1), kind=kOutput, calls=%fused_computation.20 | convolution fusion | flops 5170266112 | bytes 11960320 | tf_op jit(solution)/shard_map/dot_general | solution.py:74
  191.6 0.0 copy-done
  191.6 4.7 %copy.51 = bf16[176,8,16,128]{3,2,1,0:T(8,128)(2,1)} copy(bf16[176,8,16,128]{3,1,2,0:T(8,128)(2,1)S(1)} %fusion.13) | data formatting | bytes 11534336
  196.3 24.4 %convert_bitcast_fusion = bf16[11,64,16,128]{3,1,2,0:T(8,128)(2,1)} fusion(bf16[11,128,16,128]{3,2,1,0:T(8,128)(2,1)} %bitcast.81, f32[11,16,64]{2,1,0:T(8,128)S(1)} %fusion.39, f32[11,16,128,64]{2,3,1,0:T(8,128)} %copy-done), kind=kOutput, calls=%fused_computation.17 | convolution fusion | flops 377760896 | bytes 14462976 | tf_op jit(solution)/shard_map/chqk,ckhd->cqhd/dot_general | solution.py:38
  220.8 4.0 %copy.45 = bf16[11,64,16,128]{3,2,1,0:T(8,128)(2,1)S(1)} copy(bf16[11,64,16,128]{3,1,2,0:T(8,128)(2,1)} %convert_bitcast_fusion) | data formatting | bytes 5767168 | tf_op jit(solution)/shard_map/convert_element_type | solution.py:39
  224.8 2.7 all_to_all.33
  227.4 36.8 %all_to_all.41 = bf16[2,352,2048]{2,1,0:T(8,128)(2,1)S(1)} all-to-all(bf16[2,352,2048]{2,1,0:T(8,128)(2,1)} %all_to_all.33), channel_id=1, replica_groups=mesh['seq'=16,'head'=2] {'head'}, dimensions={0} | all-to-all | bytes 5767168 | tf_op jit(solution)/shard_map/all_to_all | solution.py:76
  264.2 1.8 copy.48
  (8 shorter events, 0.1 us)
Async XLA Ops:
  6.5 43.5 %all-gather.4.cloned.1.call-start = ((), (), s32[]{:S(2)}) async-start(), calls=%async_computation.3 | async-start | bytes 1705984 | tf_op jit(solution)/shard_map/all_gather | solution.py:20
  54.8 43.2 %all-to-all-start = ((bf16[16,2,32,896]{3,2,1,0:T(8,128)(2,1)}), bf16[16,2,32,896]{3,2,1,0:T(8,128)(2,1)S(1)}, u32[]{:S(2)}, u32[]{:S(2)}) async-start(bf16[16,2,32,896]{3,2,1,0:T(8,128)(2,1)} %broadcast_select_fusion), calls=%async_computation | async-start | bytes 3670016 | tf_op jit(solution)/shard_map/all_to_all | solution.py:66
  59.7 105.8 %all-gather.6.cloned.1.call-start = ((), (), s32[]{:S(2)}) async-start(), calls=%async_computation.4 | async-start | bytes 3784704 | tf_op jit(solution)/shard_map/all_gather | solution.py:71
  180.3 11.3 %copy-start = (f32[11,16,128,64]{2,3,1,0:T(8,128)}, f32[11,16,128,64]{2,3,1,0:T(8,128)S(1)}, u32[]{:S(2)}) copy-start(f32[11,16,128,64]{2,3,1,0:T(8,128)S(1)} %fusion.5) | copy-start | bytes 17301508
  180.3 4.1 %copy-start.1 = (bf16[896,2048]{1,0:T(8,128)(2,1)S(1)}, bf16[896,2048]{1,0:T(8,128)(2,1)}, u32[]{:S(2)}) copy-start(bf16[896,2048]{1,0:T(8,128)(2,1)} %param.10) | copy-start | bytes 11010052
  180.3 4.9 %copy-start.2 = (bf16[22,64,896]{2,1,0:T(8,128)(2,1)S(1)}, bf16[22,64,896]{2,1,0:T(8,128)(2,1)}, u32[]{:S(2)}) copy-start(bf16[22,64,896]{2,1,0:T(8,128)(2,1)} %all-gather.6.cloned.1.call-done) | copy-start | bytes 7569412
Sparse Core Ops, SparseCore 0:
  9.5 40.5 all-gather.3
  99.9 65.5 all-gather.5
where the time goes:
time: 277 us; the launch traced here: 273 us
  blocking collectives  97.3 us (35%)
  waiting for transfers between devices  80.5 us (29%)
  matrix products  45.9 us (17%)
  local copies, waits for them, and re-layouts  24.2 us (9%)
  between operations  13.6 us (5%)
  other arithmetic  6.54 us (2%)
  starting transfers between devices  4.9 us (2%)
    all_to_all x1, blocking collectives, per_device(): lax.all_to_all(queries, 'head', split_axis=1, concat_axis=0, tiled=True)  60.5 us
    all_gather x1, waiting for transfers between devices, encode_rows(): lax.all_gather(w_encoder, 'seq', axis=0, tiled=True)  39.4 us
    all_to_all x1, waiting for transfers between devices, per_device(): lax.all_to_all(outgoing, 'seq', split_axis=0, concat_axis=0, tiled=True)  38 us
    all_to_all x1, blocking collectives, per_device(): lax.all_to_all(mixed, 'head', split_axis=0, concat_axis=1, tiled=True)  36.8 us
    dot_general x1, matrix products, attend_spans(): jnp.einsum('chqk,ckhd->cqhd', probs, value_block, preferred_element_type=...  24.4 us
    unnamed x10, local copies, waits for them, and re-layouts  10.4 us
    dot_general x1, matrix products, per_device(): jnp.dot(flat_rows, w_key, preferred_element_type=jnp.float32)  8.62 us
    dot_general x1, matrix products, per_device(): jnp.dot(flat_rows, w_value, preferred_element_type=jnp.float32)  6.39 us
  transfers between devices with their start and end apart: 3, of which 3 were waited for; matrix products, arithmetic and copies ran while one was open for 2% of the time, Pallas kernels for 0%

commit v1 on v0

v1 whole, which is shorter than its diff:
```python
import functools

import jax
import jax.numpy as jnp
from jax import lax
from jax.experimental import pallas as pl
from jax.experimental.pallas import tpu as pltpu
from jax.sharding import PartitionSpec as P

HEAD_DIM = 128
SPAN = 64
NBR_LEN = 64
K_NBR = 2
DB_DEV = 8
KEYS = K_NBR * NBR_LEN
SHARERS = 4
BLOCK_HEADS = 4
EXP_SCALE = HEAD_DIM ** (-0.5) * 1.4426950408889634


def xor_permute(x, bits):
    count = lax.axis_size("seq")
    return lax.ppermute(x, "seq", [(i, i ^ bits) for i in range(count)])


def shift_heads(x, shift):
    count = lax.axis_size("head")
    return lax.ppermute(x, "head", [(i, (i + shift) % count) for i in range(count)])


def after(x, *others):
    return lax.optimization_barrier((x, *others))[0]


def encode_kernel(raw_ref, w_ref, out_ref):
    values_in = raw_ref[...].astype(jnp.float32)
    mean_square = jnp.mean(values_in * values_in, axis=-1, keepdims=True)
    normed = (values_in * lax.rsqrt(mean_square + 1e-06)).astype(jnp.bfloat16)
    summed = jnp.dot(normed, w_ref[...], preferred_element_type=jnp.float32)
    out_ref[...] = (values_in + summed / (1.0 + jnp.exp(-summed))).astype(jnp.bfloat16)


def encode_rows(raw_rows, w_encoder):
    flops = 2 * raw_rows.size * w_encoder.shape[1]
    return pl.pallas_call(
        encode_kernel,
        out_shape=jax.ShapeDtypeStruct(raw_rows.shape, raw_rows.dtype),
        compiler_params=pltpu.CompilerParams(vmem_limit_bytes=24 << 20),
        cost_estimate=pl.CostEstimate(
            flops=flops, bytes_accessed=4 * raw_rows.size + 2 * w_encoder.size, transcendentals=raw_rows.size
        ),
        name="encode",
    )(raw_rows, w_encoder)


def attend_heads(keys_of, values_of, q_ref, o_ref, qf_ref, of_ref, offset):
    rows, wide = q_ref.shape
    spans = qf_ref.shape[0] // SPAN
    qf_ref[pl.ds(offset, rows), :] = q_ref[...]
    heads = [slice(at, at + HEAD_DIM) for at in range(0, wide, HEAD_DIM)]
    places = [(slice(span * SPAN, (span + 1) * SPAN), span, cols) for cols in heads for span in range(spans)]
    scores = [
        lax.dot_general(
            qf_ref[lines, cols], keys_of(span, cols), (((1,), (1,)), ((), ())), preferred_element_type=jnp.float32
        )
        for lines, span, cols in places
    ]
    probs = []
    for score in scores:
        highest = jnp.max(score, axis=-1, keepdims=True)
        raised = jnp.exp2(score * EXP_SCALE - highest * EXP_SCALE)
        probs.append((raised * (1.0 / jnp.sum(raised, axis=-1, keepdims=True))).astype(jnp.bfloat16))
    for (lines, span, cols), prob in zip(places, probs):
        mixed = jnp.dot(prob, values_of(span, cols), preferred_element_type=jnp.float32)
        of_ref[lines, cols] = mixed.astype(jnp.bfloat16)
    o_ref[...] = of_ref[pl.ds(offset, rows), :]


def span_rows(refs, span, cols):
    tokens = KEYS // len(refs)
    return jnp.concatenate([ref[span * tokens:(span + 1) * tokens, cols] for ref in refs], axis=0)


def make_parts(enc_refs, w, made_ref):
    for part, enc_ref in enumerate(enc_refs):
        made_ref[part] = jnp.dot(enc_ref[...], w, preferred_element_type=jnp.float32).astype(jnp.bfloat16)
    return [made_ref.at[part] for part in range(len(enc_refs))]


def own_kernel(parts, info_ref, *refs):
    enc_refs = refs[:parts - 1]
    first_k, first_v, wk_ref, wv_ref, q_ref, o_ref, ks_ref, vs_ref, qf_ref, of_ref = refs[parts - 1:]
    k_refs = [first_k, *make_parts(enc_refs, wk_ref[...], ks_ref)]
    v_refs = [first_v, *make_parts(enc_refs, wv_ref[...], vs_ref)]
    attend_heads(
        functools.partial(span_rows, k_refs), functools.partial(span_rows, v_refs),
        q_ref, o_ref, qf_ref, of_ref, pl.multiple_of(info_ref[0], 16),
    )


def sent_kernel(parts, info_ref, *refs):
    enc_refs, wk_refs, wv_refs = refs[:parts], refs[parts:parts + SHARERS], refs[parts + SHARERS:parts + 2 * SHARERS]
    q_ref, _, o_ref, ks_ref, vs_ref, qf_ref, of_ref = refs[parts + 2 * SHARERS:]
    for piece in range(SHARERS):
        @pl.when(pl.program_id(0) == piece)
        def _(piece=piece):
            k_refs = make_parts(enc_refs, wk_refs[piece][...], ks_ref)
            v_refs = make_parts(enc_refs, wv_refs[piece][...], vs_ref)
            attend_heads(
                functools.partial(span_rows, k_refs), functools.partial(span_rows, v_refs),
                q_ref, o_ref, qf_ref, of_ref, pl.multiple_of(info_ref[0], 16),
            )


def cost(encoded, rows, columns):
    made = sum(part.size for part in encoded)
    return pl.CostEstimate(
        flops=4 * made * columns + 4 * rows * KEYS * columns,
        bytes_accessed=2 * made + 4 * rows * columns + 4 * encoded[0].shape[1] * columns,
        transcendentals=rows * KEYS * columns // HEAD_DIM,
    )


def scratch(parts, part_rows, spans, wide):
    return [pltpu.VMEM((parts, part_rows, wide), jnp.bfloat16)] * 2 + [
        pltpu.VMEM((spans * SPAN, wide), jnp.bfloat16)
    ] * 2


def attend_own(info, encoded, first_keys, first_values, w_key, w_value, queries, spans):
    rows, columns = queries.shape[0], w_key.shape[1]
    part_rows, enc_width = encoded[0].shape
    wide = min(BLOCK_HEADS * HEAD_DIM, columns)
    whole = pl.BlockSpec((part_rows, enc_width), lambda i, s: (0, 0))
    lines = pl.BlockSpec((part_rows, wide), lambda i, s: (0, i))
    weights = pl.BlockSpec((enc_width, wide), lambda i, s: (0, i))
    block = pl.BlockSpec((rows, wide), lambda i, s: (0, s[1] * (columns // wide) + i))
    return pl.pallas_call(
        functools.partial(own_kernel, len(encoded) + 1),
        grid_spec=pltpu.PrefetchScalarGridSpec(
            num_scalar_prefetch=1,
            grid=(columns // wide,),
            in_specs=[whole] * len(encoded) + [lines, lines, weights, weights, block],
            out_specs=block,
            scratch_shapes=scratch(len(encoded), part_rows, spans, wide),
        ),
        out_shape=jax.ShapeDtypeStruct(queries.shape, queries.dtype),
        compiler_params=pltpu.CompilerParams(vmem_limit_bytes=32 << 20),
        cost_estimate=cost(encoded, rows, columns),
        name="attend_own",
    )(info, *encoded, first_keys, first_values, w_key, w_value, queries)


def attend_sent(info, encoded, key_pieces, value_pieces, queries, out, spans):
    parts, rows = len(encoded), queries.shape[0]
    part_rows, enc_width = encoded[0].shape
    wide = key_pieces[0].shape[1]
    whole = pl.BlockSpec((part_rows, enc_width), lambda i, s: (0, 0))
    weights = pl.BlockSpec((enc_width, wide), lambda i, s: (0, 0))
    block = pl.BlockSpec((rows, wide), lambda i, s: (0, s[1 + i]))
    return pl.pallas_call(
        functools.partial(sent_kernel, parts),
        grid_spec=pltpu.PrefetchScalarGridSpec(
            num_scalar_prefetch=1,
            grid=(SHARERS,),
            in_specs=[whole] * parts + [weights] * (2 * SHARERS) + [block, pl.BlockSpec(memory_space=pl.ANY)],
            out_specs=block,
            scratch_shapes=scratch(parts, part_rows, spans, wide),
        ),
        out_shape=jax.ShapeDtypeStruct(out.shape, out.dtype),
        input_output_aliases={parts + 2 * SHARERS + 2: 0},
        compiler_params=pltpu.CompilerParams(vmem_limit_bytes=40 << 20),
        cost_estimate=cost(encoded, rows, SHARERS * wide),
        name="attend_sent",
    )(info, *encoded, *key_pieces, *value_pieces, queries, out)


def project(rows, weights):
    return jnp.dot(rows, weights, preferred_element_type=jnp.float32).astype(jnp.bfloat16)


def per_device(queries, database_rows, w_encoder, w_key, w_value, neighbour_ids):
    seq_count, head_count = lax.axis_size("seq"), lax.axis_size("head")
    seq_index, head_index = lax.axis_index("seq"), lax.axis_index("head")
    rows, group_cols = queries.shape[0], w_key.shape[1]
    half = seq_count // 2

    top, order = [half, half // 2, half + half // 2], [0, half, half // 2, half + half // 2]
    enc_blocks = jnp.stack([w_encoder, *[xor_permute(w_encoder, bits) for bits in top]])
    top_blocks, bit = enc_blocks, half // 4
    while bit:
        enc_blocks = jnp.concatenate([enc_blocks, xor_permute(enc_blocks, bit)], axis=0)
        order = order + [m ^ bit for m in order]
        bit //= 2
    place = jnp.array([order.index(m) for m in range(seq_count)], jnp.int32)
    place = place[seq_index ^ jnp.arange(seq_count, dtype=jnp.int32)]
    w_full = enc_blocks[place].reshape(-1, w_encoder.shape[1])

    by_shard = neighbour_ids.reshape(seq_count, -1)
    cited_count = by_shard.shape[1]
    cap_count = max(2, (cited_count + seq_count - 1) // seq_count)
    owners = by_shard // DB_DEV
    local_entry = by_shard % DB_DEV
    position = jnp.arange(cited_count, dtype=jnp.int32)
    same_owner = (owners[:, :, None] == owners[:, None, :]) & (
        position[None, None, :] < position[None, :, None]
    )
    earlier = jnp.sum(same_owner.astype(jnp.int32), axis=2)
    slot_index = jnp.arange(cap_count, dtype=jnp.int32)
    matches = (owners == seq_index)[:, None, :] & (earlier[:, None, :] == slot_index[None, :, None])
    source_entry = jnp.sum(jnp.where(matches, local_entry[:, None, :], 0), axis=2)
    entries = after(database_rows[source_entry], top_blocks)
    arrived = lax.all_to_all(entries, "seq", split_axis=0, concat_axis=0, tiled=True)
    flat_arrived = arrived.reshape(-1, arrived.shape[2], arrived.shape[3])
    cited_slot = lax.dynamic_index_in_dim(owners * cap_count + earlier, seq_index, 0, keepdims=False)

    shard_spans = cited_count // K_NBR
    spans = max(-(-(h * rows % SPAN + rows) // SPAN) for h in range(head_count))

    def neighbours_of(head):
        first_span = head * rows // SPAN
        span_ids = jnp.minimum(first_span + jnp.arange(spans, dtype=jnp.int32), shard_spans - 1)
        places = (span_ids[:, None] * K_NBR + jnp.arange(K_NBR, dtype=jnp.int32)).reshape(-1)
        return flat_arrived[cited_slot[places]].reshape(-1, flat_arrived.shape[2])

    received = [
        shift_heads(neighbours_of((head_index + shift) % head_count), shift) for shift in range(1, head_count)
    ]
    kept = neighbours_of(head_index)

    piece_cols = group_cols // SHARERS
    piece_index = ((seq_index >> 1) ^ (seq_index >> 2)) % 2 * 2 + seq_index % 2
    sent = []
    for shift in range(1, head_count):
        shared = []
        for weights, axis_bit in ((w_key, 2), (w_value, 4)):
            first = shift_heads(lax.dynamic_slice_in_dim(weights, piece_index * piece_cols, piece_cols, 1), shift)
            second = xor_permute(first, axis_bit)
            shared.append((first, second, xor_permute(first, 1), xor_permute(after(second, kept), 1)))
        group = (head_index - shift) % head_count
        sent.append((shared, [group * SHARERS + (piece_index ^ mask) for mask in (0, 2, 1, 3)]))

    encoded = [encode_rows(part, w_full) for part in (kept, *received)]
    offset = head_index * rows % SPAN
    framed = rows % 16 != 0
    if framed:
        frame = jnp.zeros((spans * SPAN, queries.shape[1]), queries.dtype)
        queries = lax.dynamic_update_slice_in_dim(frame, queries, offset, 0)
        first_row, offset = offset, jnp.int32(0)
    info = jnp.stack([offset, head_index]).astype(jnp.int32)
    first_keys, first_values = project(encoded[0], w_key), project(encoded[0], w_value)
    out = attend_own(info, encoded[1:], first_keys, first_values, w_key, w_value, queries, spans)
    for (key_pieces, value_pieces), blocks in sent:
        info = jnp.stack([offset, *blocks]).astype(jnp.int32)
        out = attend_sent(info, encoded, key_pieces, value_pieces, queries, out, spans)
    if framed:
        out = lax.dynamic_slice_in_dim(out, first_row, rows, 0)
    return out


def solution(mesh):
    placed = (
        P(("seq", "head"), None),
        P("seq", "head", None),
        P("seq", None),
        P(None, "head"),
        P(None, "head"),
        P(),
    )
    return jax.shard_map(
        per_device, mesh=mesh, in_specs=placed, out_specs=P(("seq", "head"), None), check_vma=False
    )
```

time: 277 us -> 111 us (0.40); the launches traced: 273 us -> 110 us
  blocking collectives: 97.3 us -> 0 us
  waiting for transfers between devices: 80.5 us -> 38.3 us
  matrix products: 45.9 us -> 5.77 us
  Pallas kernels: 0 us -> 26.9 us
  between operations: 13.6 us -> 0.39 us
  starting transfers between devices: 4.9 us -> 17.9 us
  other arithmetic: 6.54 us -> 1.06 us
  local copies, waits for them, and re-layouts: 24.2 us -> 20.1 us
    all_to_all x2 -> x0, blocking collectives: 97.3 us -> none  [the longest x1 60.5 us: per_device(): lax.all_to_all(queries, 'head', split_axis=1, concat_axis=0, tiled=True)]
    all_gather x2 -> x0, waiting for transfers between devices: 41.7 us -> none  [the longest x1 39.4 us: encode_rows(): lax.all_gather(w_encoder, 'seq', axis=0, tiled=True)]
    dot_general x5 -> x2, matrix products: 45.9 us -> 5.77 us  [project(): jnp.dot(rows, weights, preferred_element_type=jnp.float32)]
    ppermute x0 -> x14, waiting for transfers between devices: none -> 33.6 us  [the longest x11 33.6 us: xor_permute(): return lax.ppermute(x, 'seq', [(i, i ^ bits) for i in range(count)])]
    all_to_all x1, waiting for transfers between devices: 38 us -> 4.68 us  [per_device(): lax.all_to_all(entries, 'seq', split_axis=0, concat_axis=0, tiled=True)]
    pallas_call x0 -> x4, Pallas kernels: none -> 26.9 us  [the longest x1 15 us: attend_sent(): pl.pallas_call(functools.partial(sent_kernel, parts), grid_spec=pltpu.Pre...]
    ppermute x0 -> x14, starting transfers between devices: none -> 10.4 us  [the longest x11 7.52 us: xor_permute(): return lax.ppermute(x, 'seq', [(i, i ^ bits) for i in range(count)])]
    gather x2 -> x7, local copies, waits for them, and re-layouts: 2.63 us -> 11.3 us  [the longest x4 6.46 us: neighbours_of(): return flat_arrived[cited_slot[places]].reshape(-1, flat_arrived.shape[2])]
  transfers between devices with their start and end apart: 3 -> 15, of which waited for: 3 -> 4; matrix products, arithmetic and copies ran while one was open for 2% -> 24% of each run, Pallas kernels for 0% -> 11%
where the time goes in v1:
time: 111 us; the launch traced here: 110 us
  waiting for transfers between devices  38.3 us (35%)
  Pallas kernels  26.9 us (24%)
  local copies, waits for them, and re-layouts  20.1 us (18%)
  starting transfers between devices  17.9 us (16%)
  matrix products  5.77 us (5%)
    ppermute x11, waiting for transfers between devices, xor_permute(): return lax.ppermute(x, 'seq', [(i, i ^ bits) for i in range(count)])  33.6 us
    pallas_call x1, Pallas kernels, attend_sent(): pl.pallas_call(functools.partial(sent_kernel, parts), grid_spec=pltpu.Pre...  15 us
    pallas_call x1, Pallas kernels, attend_own(): pl.pallas_call(functools.partial(own_kernel, len(encoded) + 1), grid_spec...  9.65 us
    ppermute x11, starting transfers between devices, xor_permute(): return lax.ppermute(x, 'seq', [(i, i ^ bits) for i in range(count)])  7.52 us
    all_to_all x1, starting transfers between devices, per_device(): lax.all_to_all(entries, 'seq', split_axis=0, concat_axis=0, tiled=True)  7.52 us
    gather x4, local copies, waits for them, and re-layouts, neighbours_of(): return flat_arrived[cited_slot[places]].reshape(-1, flat_arrived.shape[2])  6.46 us
    dot_general x2, matrix products, project(): jnp.dot(rows, weights, preferred_element_type=jnp.float32)  5.77 us
    all_to_all x1, waiting for transfers between devices, per_device(): lax.all_to_all(entries, 'seq', split_axis=0, concat_axis=0, tiled=True)  4.68 us
  transfers between devices with their start and end apart: 15, of which 4 were waited for; matrix products, arithmetic and copies ran while one was open for 24% of the time, Pallas kernels for 11%

profile of v1, /device:TPU:3, one launch (start us, length us, event | category | flops | bytes accessed | tf_op | source)
XLA Modules:
  0.0 110.4 jit_solution(16192595746022707463)
XLA Ops:
  0.0 3.3 %collective-permute-start.2 = (bf16[56,896]{1,0:T(8,128)(2,1)}, bf16[56,896]{1,0:T(8,128)(2,1)S(1)}, u32[]{:S(2)}, u32[]{:S(2)}) collective-permute-start(bf16[56,896]{1,0:T(8,128)(2,1)} %param.9), channel_id=1, source_target_pairs={{0,24},{2,26},{4,28},{6,30},{8,16},{10,18},{12,20},{14,22},{16,8},... | collective-permute-start | bytes 301064 | tf_op jit(solution)/shard_map/ppermute | solution.py:23
  3.3 0.4 collective-permute-start.1
  3.7 1.3 %constant_dynamic-slice_fusion = bf16[896,512]{1,0:T(8,128)(2,1)S(1)} fusion(bf16[896,2048]{1,0:T(8,128)(2,1)} %refs_4_.1, s32[]{:T(128)S(6)} %select_n.156), kind=kLoop, calls=%fused_computation.51 | loop fusion | bytes 1835012 | tf_op jit(solution)/shard_map/dynamic_slice | solution.py:237
  4.9 1.3 %collective-permute-start.10 = (bf16[896,512]{1,0:T(8,128)(2,1)S(1)}, bf16[896,512]{1,0:T(8,128)(2,1)}, u32[]{:S(2)}, u32[]{:S(2)}) collective-permute-start(bf16[896,512]{1,0:T(8,128)(2,1)S(1)} %constant_dynamic-slice_fusion), channel_id=1, source_target_pairs={{0,1},{1,0},{2,3},{3,2},{4,5},{5,4},{6,7},{7,6},{8,9},{9,8},{10,11... | collective-permute-start | bytes 2752520 | tf_op jit(solution)/shard_map/ppermute | solution.py:28
  6.2 1.2 %constant_dynamic-slice_fusion.1 = bf16[896,512]{1,0:T(8,128)(2,1)S(1)} fusion(bf16[896,2048]{1,0:T(8,128)(2,1)} %refs_3_.1, s32[]{:T(128)S(6)} %select_n.156), kind=kLoop, calls=%fused_computation.52 | loop fusion | bytes 1835012 | tf_op jit(solution)/shard_map/dynamic_slice | solution.py:237
  7.5 0.3 collective-permute-start.6
  7.8 0.1 copy.32
  7.9 0.1 reshape.260
  8.1 0.1 copy.33
  8.1 0.5 convert_reduce_fusion
  8.8 0.1 select_reduce_fusion
  8.9 0.1 copy.35
  9.0 0.1 reshape.267
  9.1 2.0 %gather_fusion = bf16[32,32,896]{2,1,0:T(8,128)(2,1)} fusion(bf16[8,32,896]{2,1,0:T(8,128)(2,1)S(1)} %copy-done, s32[1024]{0:T(1024)S(1)} %pad_clamp_fusion.6), kind=kCustom, calls=%fused_computation | custom fusion | bytes 3670144 | tf_op jit(solution)/shard_map/gather | solution.py:212
  11.1 0.5 collective-permute-done
  11.6 7.5 %all-to-all-start = ((bf16[16,2,32,896]{3,2,1,0:T(8,128)(2,1)}), bf16[16,2,32,896]{3,2,1,0:T(8,128)(2,1)}, u32[]{:S(2)}, u32[]{:S(2)}) async-start(bf16[16,2,32,896]{3,2,1,0:T(8,128)(2,1)} %bitcast.6), calls=%async_computation | async-start | bytes 3670016 | tf_op jit(solution)/shard_map/all_to_all | solution.py:213
  19.2 0.1 add.242
  19.4 0.1 add.230
  19.5 0.7 gather_fusion.5
  20.2 0.7 constant_dynamic-update-slice_fusion.4
  20.9 0.1 collective-permute-start.3
  21.0 0.7 constant_dynamic-update-slice_fusion.3
  21.7 0.7 constant_dynamic-update-slice_fusion.2
  22.4 0.7 constant_dynamic-update-slice_fusion.1
  23.1 21.1 %collective-permute-done.3 = bf16[4,56,896]{2,1,0:T(8,128)(2,1)S(1)} collective-permute-done((bf16[4,56,896]{2,1,0:T(8,128)(2,1)S(1)}, bf16[4,56,896]{2,1,0:T(8,128)(2,1)S(1)}, u32[]{:S(2)}, u32[]{:S(2)}) %collective-permute-start.3) | collective-permute-done | bytes 401440 | tf_op jit(solution)/shard_map/ppermute | solution.py:23
  44.2 1.0 constant_dynamic-update-slice_fusion
  45.2 1.1 %collective-permute-start.4 = (bf16[8,56,896]{2,1,0:T(8,128)(2,1)}, bf16[8,56,896]{2,1,0:T(8,128)(2,1)S(1)}, u32[]{:S(2)}, u32[]{:S(2)}) collective-permute-start(bf16[8,56,896]{2,1,0:T(8,128)(2,1)} %get-tuple-element.13), channel_id=1, source_target_pairs={{0,2},{2,0},{4,6},{6,4},{8,10},{10,8},{12,14},{14,12},{16,18},{18,... | collective-permute-start | bytes 2408456 | tf_op jit(solution)/shard_map/ppermute | solution.py:23
  46.4 0.6 collective-permute-start.7
  47.0 0.7 gather_fusion.1
  47.7 0.7 gather_fusion.3
  48.4 0.1 stack.45.info_ref
  48.5 1.2 %collective-permute-start.12 = (bf16[896,512]{1,0:T(8,128)(2,1)}, bf16[896,512]{1,0:T(8,128)(2,1)}, u32[]{:S(2)}, u32[]{:S(2)}) collective-permute-start(bf16[896,512]{1,0:T(8,128)(2,1)} %collective-permute-done.10.refs_6_), channel_id=1, source_target_pairs={{0,2},{2,0},{4,6},{6,4},{8,10},{10,8},{12,14},{14,12},{16,18},{18,... | collective-permute-start | bytes 2752520 | tf_op jit(solution)/shard_map/ppermute | solution.py:23
  49.7 0.1 collective-permute-start.8
  49.8 1.0 constant_dynamic-update-slice_fusion.5
  50.7 2.2 %gather_fusion.4 = bf16[16,56,896]{2,1,0:T(8,128)(2,1)S(1)} fusion(bf16[16,56,896]{2,1,0:T(8,128)(2,1)} %constant_dynamic-update-slice_fusion.5, s32[1024]{0:T(1024)S(1)} %pad_clamp_fusion.2), kind=kCustom, calls=%fused_computation.4 | custom fusion | bytes 3211328 | tf_op jit(solution)/shard_map/gather | solution.py:197
  53.0 4.7 %all-to-all-done = bf16[16,2,32,896]{3,2,1,0:T(8,128)(2,1)} async-done(((bf16[16,2,32,896]{3,2,1,0:T(8,128)(2,1)}), bf16[16,2,32,896]{3,2,1,0:T(8,128)(2,1)}, u32[]{:S(2)}, u32[]{:S(2)}) %all-to-all-start) | async-done | bytes 1835040 | tf_op jit(solution)/shard_map/all_to_all | solution.py:213
  57.7 3.0 %gather_fusion.6 = bf16[12,32,896]{2,1,0:T(8,128)(2,1)} fusion(bf16[32,32,896]{2,1,0:T(8,128)(2,1)} %bitcast.11, s32[1024]{0:T(1024)S(1)} %pad_clamp_fusion), kind=kCustom, calls=%fused_computation.6 | custom fusion | bytes 1376304 | tf_op jit(solution)/shard_map/gather | solution.py:224
  60.7 1.2 %collective-permute-start.5 = (bf16[384,896]{1,0:T(8,128)(2,1)}, bf16[384,896]{1,0:T(8,128)(2,1)S(1)}, u32[]{:S(2)}, u32[]{:S(2)}) collective-permute-start(bf16[384,896]{1,0:T(8,128)(2,1)} %bitcast.24), channel_id=1, source_target_pairs={{0,1},{1,0},{2,3},{3,2},{4,5},{5,4},{6,7},{7,6},{8,9},{9,8},{10,11... | collective-permute-start | bytes 2064392 | tf_op jit(solution)/shard_map/ppermute | solution.py:28
  61.9 2.2 %gather_fusion.2 = bf16[12,32,896]{2,1,0:T(8,128)(2,1)S(1)} fusion(bf16[32,32,896]{2,1,0:T(8,128)(2,1)} %bitcast.11, s32[1024]{0:T(1024)S(1)} %pad_clamp_fusion.4), kind=kCustom, calls=%fused_computation.2 | custom fusion | bytes 1376304 | tf_op jit(solution)/shard_map/gather | solution.py:224
  64.1 12.1 %collective-permute-done.11.refs_7_ = bf16[896,512]{1,0:T(8,128)(2,1)} collective-permute-done((bf16[896,512]{1,0:T(8,128)(2,1)}, bf16[896,512]{1,0:T(8,128)(2,1)}, u32[]{:S(2)}, u32[]{:S(2)}) %collective-permute-start.11) | collective-permute-done | bytes 917536 | tf_op jit(solution)/shard_map/ppermute | solution.py:23
  76.1 0.7 collective-permute-start.13
  76.8 1.1 %encode.2.refs_0_ = bf16[384,896]{1,0:T(8,128)(2,1)S(1)} custom-call(bf16[384,896]{1,0:T(8,128)(2,1)S(1)} %bitcast.53, bf16[896,896]{1,0:T(8,128)(2,1)S(1)} %bitcast.51), custom_call_target="tpu_custom_call" | custom-call | flops 616562688 | bytes 2981888 | tf_op jit(solution)/shard_map/encode/pallas_call | solution.py:45
  78.1 4.0 %convolution_convert_fusion.refs_2_ = bf16[384,2048]{1,0:T(8,128)(2,1)S(1)} fusion(bf16[384,896]{1,0:T(8,128)(2,1)S(1)} %encode.2.refs_0_, bf16[896,2048]{1,0:T(8,128)(2,1)} %refs_4_.1), kind=kOutput, calls=%fused_computation.7 | convolution fusion | flops 1410072576 | bytes 5931008 | tf_op jit(solution)/shard_map/dot_general | solution.py:179
  82.1 1.8 %convolution_convert_fusion.1.refs_1_ = bf16[384,2048]{1,0:T(8,128)(2,1)S(1)} fusion(bf16[384,896]{1,0:T(8,128)(2,1)S(1)} %encode.2.refs_0_, bf16[896,2048]{1,0:T(8,128)(2,1)S(1)} %copy-done.1), kind=kOutput, calls=%fused_computation.8 | convolution fusion | flops 1410072576 | bytes 5931008 | tf_op jit(solution)/shard_map/dot_general | solution.py:179
  83.9 1.1 %encode.3.refs_0_.refs_1_ = bf16[384,896]{1,0:T(8,128)(2,1)S(1)} custom-call(bf16[384,896]{1,0:T(8,128)(2,1)S(1)} %collective-permute-done.5.raw_ref, bf16[896,896]{1,0:T(8,128)(2,1)S(1)} %bitcast.52), custom_call_target="tpu_custom_call" | custom-call | flops 616562688 | bytes 2981888 | tf_op jit(solution)/shard_map/encode/pallas_call | solution.py:45
  85.1 0.7 copy-done.3
  85.7 9.7 %attend_own.1.refs_11_ = bf16[352,4096]{1,0:T(8,128)(2,1)} custom-call(s32[2]{0:T(128)S(1)} %pad_add_fusion.info_ref, bf16[384,896]{1,0:T(8,128)(2,1)S(1)} %encode.3.refs_0_.refs_1_, bf16[384,2048]{1,0:T(8,128)(2,1)S(1)} %convolution_convert_fusion.1.refs_1_, bf16[384,2048]{1,0:T(8,128)(2,1)S(1)} %convolution_convert_fusion.refs_2_, ...), custom_call_target="tpu_custom_call" | custom-call | flops 3187671040 | bytes 10911744 | tf_op jit(solution)/shard_map/attend_own/pallas_call | solution.py:138
  95.4 15.0 %attend_sent.1 = bf16[352,4096]{1,0:T(8,128)(2,1)} custom-call(s32[5]{0:T(128)S(1)} %stack.45.info_ref, bf16[384,896]{1,0:T(8,128)(2,1)S(1)} %encode.2.refs_0_, bf16[384,896]{1,0:T(8,128)(2,1)S(1)} %encode.3.refs_0_.refs_1_, bf16[896,512]{1,0:T(8,128)(2,1)} %collective-permute-done.6.refs_2_, ...), custom_call_target="tpu_custom_call", output_to_operand_aliasing={{}: (12, {})} | custom-call | flops 6006243328 | bytes 11599872 | tf_op jit(solution)/shard_map/attend_sent/pallas_call | solution.py:161
  (51 shorter events, 0.7 us)
Async XLA Ops:
  0.0 9.1 %copy-start = (bf16[8,32,896]{2,1,0:T(8,128)(2,1)S(1)}, bf16[8,32,896]{2,1,0:T(8,128)(2,1)}, u32[]{:S(2)}) copy-start(bf16[8,32,896]{2,1,0:T(8,128)(2,1)} %param.8) | copy-start | bytes 1376260
  0.0 11.1 %collective-permute-start.2 = (bf16[56,896]{1,0:T(8,128)(2,1)}, bf16[56,896]{1,0:T(8,128)(2,1)S(1)}, u32[]{:S(2)}, u32[]{:S(2)}) collective-permute-start(bf16[56,896]{1,0:T(8,128)(2,1)} %param.9), channel_id=1, source_target_pairs={{0,24},{2,26},{4,28},{6,30},{8,16},{10,18},{12,20},{14,22},{16,8},... | collective-permute-start | bytes 301064 | tf_op jit(solution)/shard_map/ppermute | solution.py:23
  3.3 8.2 %collective-permute-start = (bf16[56,896]{1,0:T(8,128)(2,1)}, bf16[56,896]{1,0:T(8,128)(2,1)S(1)}, u32[]{:S(2)}, u32[]{:S(2)}) collective-permute-start(bf16[56,896]{1,0:T(8,128)(2,1)} %param.9), channel_id=1, source_target_pairs={{0,16},{2,18},{4,20},{6,22},{8,24},{10,26},{12,28},{14,30},{16,0},... | collective-permute-start | bytes 301064 | tf_op jit(solution)/shard_map/ppermute | solution.py:23
  3.3 8.2 %collective-permute-start.1 = (bf16[56,896]{1,0:T(8,128)(2,1)}, bf16[56,896]{1,0:T(8,128)(2,1)S(1)}, u32[]{:S(2)}, u32[]{:S(2)}) collective-permute-start(bf16[56,896]{1,0:T(8,128)(2,1)} %param.9), channel_id=1, source_target_pairs={{0,8},{2,10},{4,12},{6,14},{8,0},{10,2},{12,4},{14,6},{16,24},{18,... | collective-permute-start | bytes 301064 | tf_op jit(solution)/shard_map/ppermute | solution.py:23
  3.7 4.1 %copy-start.6 = (s32[176,2]{0,1:T(2,128)S(1)}, s32[176,2]{0,1:T(2,128)}, u32[]{:S(2)}) copy-start(s32[176,2]{0,1:T(2,128)} %param.12) | copy-start | bytes 4228
  4.9 41.4 %collective-permute-start.10 = (bf16[896,512]{1,0:T(8,128)(2,1)S(1)}, bf16[896,512]{1,0:T(8,128)(2,1)}, u32[]{:S(2)}, u32[]{:S(2)}) collective-permute-start(bf16[896,512]{1,0:T(8,128)(2,1)S(1)} %constant_dynamic-slice_fusion), channel_id=1, source_target_pairs={{0,1},{1,0},{2,3},{3,2},{4,5},{5,4},{6,7},{7,6},{8,9},{9,8},{10,11... | collective-permute-start | bytes 2752520 | tf_op jit(solution)/shard_map/ppermute | solution.py:28
  7.5 38.9 %collective-permute-start.6 = (bf16[896,512]{1,0:T(8,128)(2,1)S(1)}, bf16[896,512]{1,0:T(8,128)(2,1)}, u32[]{:S(2)}, u32[]{:S(2)}) collective-permute-start(bf16[896,512]{1,0:T(8,128)(2,1)S(1)} %constant_dynamic-slice_fusion.1), channel_id=1, source_target_pairs={{0,1},{1,0},{2,3},{3,2},{4,5},{5,4},{6,7},{7,6},{8,9},{9,8},{10,11... | collective-permute-start | bytes 2752520 | tf_op jit(solution)/shard_map/ppermute | solution.py:28
  9.1 2.5 %copy-start.5 = (bf16[56,896]{1,0:T(8,128)(2,1)S(1)}, bf16[56,896]{1,0:T(8,128)(2,1)}, u32[]{:S(2)}) copy-start(bf16[56,896]{1,0:T(8,128)(2,1)} %param.9) | copy-start | bytes 301060
  11.6 46.0 %all-to-all-start = ((bf16[16,2,32,896]{3,2,1,0:T(8,128)(2,1)}), bf16[16,2,32,896]{3,2,1,0:T(8,128)(2,1)}, u32[]{:S(2)}, u32[]{:S(2)}) async-start(bf16[16,2,32,896]{3,2,1,0:T(8,128)(2,1)} %bitcast.6), calls=%async_computation | async-start | bytes 3670016 | tf_op jit(solution)/shard_map/all_to_all | solution.py:213
  20.2 27.6 %copy-start.4 = (s32[16]{0:T(128)S(1)}, s32[16]{0:T(128)}, u32[]{:S(2)}) copy-start(s32[16]{0:T(128)} %constant.119.clone) | copy-start | bytes 196
  20.9 23.3 %collective-permute-start.3 = (bf16[4,56,896]{2,1,0:T(8,128)(2,1)S(1)}, bf16[4,56,896]{2,1,0:T(8,128)(2,1)S(1)}, u32[]{:S(2)}, u32[]{:S(2)}) collective-permute-start(bf16[4,56,896]{2,1,0:T(8,128)(2,1)S(1)} %pad_maximum_fusion), channel_id=1, source_target_pairs={{0,4},{2,6},{4,0},{6,2},{8,12},{10,14},{12,8},{14,10},{16,20},{18,... | collective-permute-start | bytes 1204232 | tf_op jit(solution)/shard_map/ppermute | solution.py:23
  45.2 4.6 %collective-permute-start.4 = (bf16[8,56,896]{2,1,0:T(8,128)(2,1)}, bf16[8,56,896]{2,1,0:T(8,128)(2,1)S(1)}, u32[]{:S(2)}, u32[]{:S(2)}) collective-permute-start(bf16[8,56,896]{2,1,0:T(8,128)(2,1)} %get-tuple-element.13), channel_id=1, source_target_pairs={{0,2},{2,0},{4,6},{6,4},{8,10},{10,8},{12,14},{14,12},{16,18},{18,... | collective-permute-start | bytes 2408456 | tf_op jit(solution)/shard_map/ppermute | solution.py:23
  46.3 29.9 %collective-permute-start.11 = (bf16[896,512]{1,0:T(8,128)(2,1)}, bf16[896,512]{1,0:T(8,128)(2,1)}, u32[]{:S(2)}, u32[]{:S(2)}) collective-permute-start(bf16[896,512]{1,0:T(8,128)(2,1)} %collective-permute-done.10.refs_6_), channel_id=1, source_target_pairs={{0,8},{2,10},{4,12},{6,14},{8,0},{10,2},{12,4},{14,6},{16,24},{18,... | collective-permute-start | bytes 2752520 | tf_op jit(solution)/shard_map/ppermute | solution.py:23
  46.4 31.6 %collective-permute-start.7 = (bf16[896,512]{1,0:T(8,128)(2,1)}, bf16[896,512]{1,0:T(8,128)(2,1)}, u32[]{:S(2)}, u32[]{:S(2)}) collective-permute-start(bf16[896,512]{1,0:T(8,128)(2,1)} %collective-permute-done.6.refs_2_), channel_id=1, source_target_pairs={{0,4},{2,6},{4,0},{6,2},{8,12},{10,14},{12,8},{14,10},{16,20},{18,... | collective-permute-start | bytes 2752520 | tf_op jit(solution)/shard_map/ppermute | solution.py:23
  48.5 46.9 %collective-permute-start.12 = (bf16[896,512]{1,0:T(8,128)(2,1)}, bf16[896,512]{1,0:T(8,128)(2,1)}, u32[]{:S(2)}, u32[]{:S(2)}) collective-permute-start(bf16[896,512]{1,0:T(8,128)(2,1)} %collective-permute-done.10.refs_6_), channel_id=1, source_target_pairs={{0,2},{2,0},{4,6},{6,4},{8,10},{10,8},{12,14},{14,12},{16,18},{18,... | collective-permute-start | bytes 2752520 | tf_op jit(solution)/shard_map/ppermute | solution.py:23
  49.7 45.7 %collective-permute-start.8 = (bf16[896,512]{1,0:T(8,128)(2,1)}, bf16[896,512]{1,0:T(8,128)(2,1)}, u32[]{:S(2)}, u32[]{:S(2)}) collective-permute-start(bf16[896,512]{1,0:T(8,128)(2,1)} %collective-permute-done.6.refs_2_), channel_id=1, source_target_pairs={{0,2},{2,0},{4,6},{6,4},{8,10},{10,8},{12,14},{14,12},{16,18},{18,... | collective-permute-start | bytes 2752520 | tf_op jit(solution)/shard_map/ppermute | solution.py:23
  60.7 23.2 %collective-permute-start.5 = (bf16[384,896]{1,0:T(8,128)(2,1)}, bf16[384,896]{1,0:T(8,128)(2,1)S(1)}, u32[]{:S(2)}, u32[]{:S(2)}) collective-permute-start(bf16[384,896]{1,0:T(8,128)(2,1)} %bitcast.24), channel_id=1, source_target_pairs={{0,1},{1,0},{2,3},{3,2},{4,5},{5,4},{6,7},{7,6},{8,9},{9,8},{10,11... | collective-permute-start | bytes 2064392 | tf_op jit(solution)/shard_map/ppermute | solution.py:28
  76.1 19.3 %collective-permute-start.13 = (bf16[896,512]{1,0:T(8,128)(2,1)}, bf16[896,512]{1,0:T(8,128)(2,1)S(1)}, u32[]{:S(2)}, u32[]{:S(2)}) collective-permute-start(bf16[896,512]{1,0:T(8,128)(2,1)} %collective-permute-done.11.refs_7_), channel_id=1, source_target_pairs={{0,2},{2,0},{4,6},{6,4},{8,10},{10,8},{12,14},{14,12},{16,18},{18,... | collective-permute-start | bytes 2752520 | tf_op jit(solution)/shard_map/ppermute | solution.py:23
  78.0 4.1 %copy-start.1 = (bf16[896,2048]{1,0:T(8,128)(2,1)S(1)}, bf16[896,2048]{1,0:T(8,128)(2,1)}, u32[]{:S(2)}) copy-start(bf16[896,2048]{1,0:T(8,128)(2,1)} %refs_3_.1) | copy-start | bytes 11010052
  78.0 17.4 %collective-permute-start.9 = (bf16[896,512]{1,0:T(8,128)(2,1)}, bf16[896,512]{1,0:T(8,128)(2,1)S(1)}, u32[]{:S(2)}, u32[]{:S(2)}) collective-permute-start(bf16[896,512]{1,0:T(8,128)(2,1)} %collective-permute-done.7.refs_3_), channel_id=1, source_target_pairs={{0,2},{2,0},{4,6},{6,4},{8,10},{10,8},{12,14},{14,12},{16,18},{18,... | collective-permute-start | bytes 2752520 | tf_op jit(solution)/shard_map/ppermute | solution.py:23
  82.1 3.0 %copy-start.2 = (bf16[896,2048]{1,0:T(8,128)(2,1)S(1)}, bf16[896,2048]{1,0:T(8,128)(2,1)}, u32[]{:S(2)}) copy-start(bf16[896,2048]{1,0:T(8,128)(2,1)} %refs_4_.1) | copy-start | bytes 11010052
  83.9 1.9 %copy-start.3 = (bf16[352,4096]{1,0:T(8,128)(2,1)S(1)}, bf16[352,4096]{1,0:T(8,128)(2,1)}, u32[]{:S(2)}) copy-start(bf16[352,4096]{1,0:T(8,128)(2,1)} %refs_10_.1) | copy-start | bytes 8650756

commit v2 on v1

--- a/solution.py
+++ b/solution.py
@@ -90,8 +90,10 @@
 def own_kernel(parts, info_ref, *refs):
     enc_refs = refs[:parts - 1]
     first_k, first_v, wk_ref, wv_ref, q_ref, o_ref, ks_ref, vs_ref, qf_ref, of_ref = refs[parts - 1:]
-    k_refs = [first_k, *make_parts(enc_refs, wk_ref[...], ks_ref)]
-    v_refs = [first_v, *make_parts(enc_refs, wv_ref[...], vs_ref)]
+    wide = q_ref.shape[1]
+    here = pl.ds(pl.multiple_of(pl.program_id(0) * wide, wide), wide)
+    k_refs = [first_k.at[:, here], *make_parts(enc_refs, wk_ref[:, here], ks_ref)]
+    v_refs = [first_v.at[:, here], *make_parts(enc_refs, wv_ref[:, here], vs_ref)]
     attend_heads(
         functools.partial(span_rows, k_refs), functools.partial(span_rows, v_refs),
         q_ref, o_ref, qf_ref, of_ref, pl.multiple_of(info_ref[0], 16),
@@ -131,16 +133,14 @@
     rows, columns = queries.shape[0], w_key.shape[1]
     part_rows, enc_width = encoded[0].shape
     wide = min(BLOCK_HEADS * HEAD_DIM, columns)
-    whole = pl.BlockSpec((part_rows, enc_width), lambda i, s: (0, 0))
-    lines = pl.BlockSpec((part_rows, wide), lambda i, s: (0, i))
-    weights = pl.BlockSpec((enc_width, wide), lambda i, s: (0, i))
+    whole = pl.BlockSpec(memory_space=pltpu.VMEM)
     block = pl.BlockSpec((rows, wide), lambda i, s: (0, s[1] * (columns // wide) + i))
     return pl.pallas_call(
         functools.partial(own_kernel, len(encoded) + 1),
         grid_spec=pltpu.PrefetchScalarGridSpec(
             num_scalar_prefetch=1,
             grid=(columns // wide,),
-            in_specs=[whole] * len(encoded) + [lines, lines, weights, weights, block],
+            in_specs=[whole] * (len(encoded) + 4) + [block],
             out_specs=block,
             scratch_shapes=scratch(len(encoded), part_rows, spans, wide),
         ),
@@ -228,6 +228,8 @@
     ]
     kept = neighbours_of(head_index)
 
+    encoded = [encode_rows(part, w_full) for part in (kept, *received)]
+    own_keys, own_values = project(encoded[0], w_key), project(encoded[0], w_value)
     piece_cols = group_cols // SHARERS
     piece_index = ((seq_index >> 1) ^ (seq_index >> 2)) % 2 * 2 + seq_index % 2
     sent = []
@@ -236,11 +238,10 @@
         for weights, axis_bit in ((w_key, 2), (w_value, 4)):
             first = shift_heads(lax.dynamic_slice_in_dim(weights, piece_index * piece_cols, piece_cols, 1), shift)
             second = xor_permute(first, axis_bit)
-            shared.append((first, second, xor_permute(first, 1), xor_permute(after(second, kept), 1)))
+            shared.append((first, second, xor_permute(first, 1), xor_permute(after(second, own_values), 1)))
         group = (head_index - shift) % head_count
         sent.append((shared, [group * SHARERS + (piece_index ^ mask) for mask in (0, 2, 1, 3)]))
 
-    encoded = [encode_rows(part, w_full) for part in (kept, *received)]
     offset = head_index * rows % SPAN
     framed = rows % 16 != 0
     if framed:
@@ -248,8 +249,7 @@
         queries = lax.dynamic_update_slice_in_dim(frame, queries, offset, 0)
         first_row, offset = offset, jnp.int32(0)
     info = jnp.stack([offset, head_index]).astype(jnp.int32)
-    first_keys, first_values = project(encoded[0], w_key), project(encoded[0], w_value)
-    out = attend_own(info, encoded[1:], first_keys, first_values, w_key, w_value, queries, spans)
+    out = attend_own(info, encoded[1:], own_keys, own_values, w_key, w_value, queries, spans)
     for (key_pieces, value_pieces), blocks in sent:
         info = jnp.stack([offset, *blocks]).astype(jnp.int32)
         out = attend_sent(info, encoded, key_pieces, value_pieces, queries, out, spans)

time: 111 us -> 107 us (0.964); the launches traced: 110 us -> 105 us
  waiting for transfers between devices: 38.3 us -> 34.9 us
    ppermute x11, waiting for transfers between devices: 33.6 us -> 29.4 us  [xor_permute(): return lax.ppermute(x, 'seq', [(i, i ^ bits) for i in range(count)])]
  transfers between devices with their start and end apart: 15 -> 15, of which waited for: 4 -> 4; matrix products, arithmetic and copies ran while one was open for 24% -> 25% of each run, Pallas kernels for 11% -> 11%
where the time goes in v2:
time: 107 us; the launch traced here: 105 us
  waiting for transfers between devices  34.9 us (33%)
  Pallas kernels  26.2 us (24%)
  local copies, waits for them, and re-layouts  20.1 us (19%)
  starting transfers between devices  17 us (16%)
  matrix products  5.77 us (5%)
    ppermute x11, waiting for transfers between devices, xor_permute(): return lax.ppermute(x, 'seq', [(i, i ^ bits) for i in range(count)])  29.4 us
    pallas_call x1, Pallas kernels, attend_sent(): pl.pallas_call(functools.partial(sent_kernel, parts), grid_spec=pltpu.Pre...  15 us
    pallas_call x1, Pallas kernels, attend_own(): pl.pallas_call(functools.partial(own_kernel, len(encoded) + 1), grid_spec...  8.88 us
    all_to_all x1, starting transfers between devices, per_device(): lax.all_to_all(entries, 'seq', split_axis=0, concat_axis=0, tiled=True)  7.52 us
    ppermute x11, starting transfers between devices, xor_permute(): return lax.ppermute(x, 'seq', [(i, i ^ bits) for i in range(count)])  6.62 us
    gather x4, local copies, waits for them, and re-layouts, neighbours_of(): return flat_arrived[cited_slot[places]].reshape(-1, flat_arrived.shape[2])  6.46 us
    dot_general x2, matrix products, project(): jnp.dot(rows, weights, preferred_element_type=jnp.float32)  5.77 us
    all_to_all x1, waiting for transfers between devices, per_device(): lax.all_to_all(entries, 'seq', split_axis=0, concat_axis=0, tiled=True)  5.45 us
  transfers between devices with their start and end apart: 15, of which 4 were waited for; matrix products, arithmetic and copies ran while one was open for 25% of the time, Pallas kernels for 11%

profile of v2, /device:TPU:3, one launch (start us, length us, event | category | flops | bytes accessed | tf_op | source)
XLA Modules:
  0.0 105.2 jit_solution(16519398496884504846)
XLA Ops:
  0.0 3.3 %collective-permute-start.2 = (bf16[56,896]{1,0:T(8,128)(2,1)}, bf16[56,896]{1,0:T(8,128)(2,1)S(1)}, u32[]{:S(2)}, u32[]{:S(2)}) collective-permute-start(bf16[56,896]{1,0:T(8,128)(2,1)} %param.9), channel_id=1, source_target_pairs={{0,24},{2,26},{4,28},{6,30},{8,16},{10,18},{12,20},{14,22},{16,8},... | collective-permute-start | bytes 301064 | tf_op jit(solution)/shard_map/ppermute | solution.py:23
  3.3 0.4 collective-permute-start.1
  3.7 1.3 %constant_dynamic-slice_fusion = bf16[896,512]{1,0:T(8,128)(2,1)S(1)} fusion(bf16[896,2048]{1,0:T(8,128)(2,1)} %refs_4_.1, s32[]{:T(128)S(6)} %select_n.156), kind=kLoop, calls=%fused_computation.51 | loop fusion | bytes 1835012 | tf_op jit(solution)/shard_map/dynamic_slice | solution.py:239
  4.9 1.3 %collective-permute-start.10 = (bf16[896,512]{1,0:T(8,128)(2,1)S(1)}, bf16[896,512]{1,0:T(8,128)(2,1)}, u32[]{:S(2)}, u32[]{:S(2)}) collective-permute-start(bf16[896,512]{1,0:T(8,128)(2,1)S(1)} %constant_dynamic-slice_fusion), channel_id=1, source_target_pairs={{0,1},{1,0},{2,3},{3,2},{4,5},{5,4},{6,7},{7,6},{8,9},{9,8},{10,11... | collective-permute-start | bytes 2752520 | tf_op jit(solution)/shard_map/ppermute | solution.py:28
  6.2 1.2 %constant_dynamic-slice_fusion.1 = bf16[896,512]{1,0:T(8,128)(2,1)S(1)} fusion(bf16[896,2048]{1,0:T(8,128)(2,1)} %refs_3_.1, s32[]{:T(128)S(6)} %select_n.156), kind=kLoop, calls=%fused_computation.52 | loop fusion | bytes 1835012 | tf_op jit(solution)/shard_map/dynamic_slice | solution.py:239
  7.5 0.3 collective-permute-start.6
  7.8 0.1 copy.32
  7.9 0.1 reshape.260
  8.1 0.1 copy.33
  8.1 0.5 convert_reduce_fusion
  8.8 0.1 select_reduce_fusion
  8.9 0.1 copy.35
  9.0 0.1 reshape.267
  9.1 2.0 %gather_fusion = bf16[32,32,896]{2,1,0:T(8,128)(2,1)} fusion(bf16[8,32,896]{2,1,0:T(8,128)(2,1)S(1)} %copy-done, s32[1024]{0:T(1024)S(1)} %pad_clamp_fusion.6), kind=kCustom, calls=%fused_computation | custom fusion | bytes 3670144 | tf_op jit(solution)/shard_map/gather | solution.py:212
  11.1 0.5 collective-permute-done
  11.6 7.5 %all-to-all-start = ((bf16[16,2,32,896]{3,2,1,0:T(8,128)(2,1)}), bf16[16,2,32,896]{3,2,1,0:T(8,128)(2,1)}, u32[]{:S(2)}, u32[]{:S(2)}) async-start(bf16[16,2,32,896]{3,2,1,0:T(8,128)(2,1)} %bitcast.6), calls=%async_computation | async-start | bytes 3670016 | tf_op jit(solution)/shard_map/all_to_all | solution.py:213
  19.2 0.1 add.242
  19.4 0.1 add.230
  19.5 0.7 gather_fusion.5
  20.2 0.7 constant_dynamic-update-slice_fusion.4
  20.9 0.1 collective-permute-start.3
  21.0 0.7 constant_dynamic-update-slice_fusion.3
  21.7 0.7 constant_dynamic-update-slice_fusion.2
  22.4 0.7 constant_dynamic-update-slice_fusion.1
  23.1 21.1 %collective-permute-done.3 = bf16[4,56,896]{2,1,0:T(8,128)(2,1)S(1)} collective-permute-done((bf16[4,56,896]{2,1,0:T(8,128)(2,1)S(1)}, bf16[4,56,896]{2,1,0:T(8,128)(2,1)S(1)}, u32[]{:S(2)}, u32[]{:S(2)}) %collective-permute-start.3) | collective-permute-done | bytes 401440 | tf_op jit(solution)/shard_map/ppermute | solution.py:23
  44.2 1.0 constant_dynamic-update-slice_fusion
  45.2 1.1 %collective-permute-start.4 = (bf16[8,56,896]{2,1,0:T(8,128)(2,1)}, bf16[8,56,896]{2,1,0:T(8,128)(2,1)S(1)}, u32[]{:S(2)}, u32[]{:S(2)}) collective-permute-start(bf16[8,56,896]{2,1,0:T(8,128)(2,1)} %get-tuple-element.13), channel_id=1, source_target_pairs={{0,2},{2,0},{4,6},{6,4},{8,10},{10,8},{12,14},{14,12},{16,18},{18,... | collective-permute-start | bytes 2408456 | tf_op jit(solution)/shard_map/ppermute | solution.py:23
  46.3 0.7 gather_fusion.1
  47.0 0.7 gather_fusion.3
  47.7 0.6 collective-permute-start.7
  48.3 0.1 stack.45.info_ref
  48.4 0.4 collective-permute-start.12
  48.8 0.2 collective-permute-start.8
  49.0 1.0 constant_dynamic-update-slice_fusion.5
  50.0 2.2 %gather_fusion.4 = bf16[16,56,896]{2,1,0:T(8,128)(2,1)S(1)} fusion(bf16[16,56,896]{2,1,0:T(8,128)(2,1)} %constant_dynamic-update-slice_fusion.5, s32[1024]{0:T(1024)S(1)} %pad_clamp_fusion.2), kind=kCustom, calls=%fused_computation.4 | custom fusion | bytes 3211328 | tf_op jit(solution)/shard_map/gather | solution.py:197
  52.2 5.4 %all-to-all-done = bf16[16,2,32,896]{3,2,1,0:T(8,128)(2,1)} async-done(((bf16[16,2,32,896]{3,2,1,0:T(8,128)(2,1)}), bf16[16,2,32,896]{3,2,1,0:T(8,128)(2,1)}, u32[]{:S(2)}, u32[]{:S(2)}) %all-to-all-start) | async-done | bytes 1835040 | tf_op jit(solution)/shard_map/all_to_all | solution.py:213
  57.7 3.0 %gather_fusion.6 = bf16[12,32,896]{2,1,0:T(8,128)(2,1)} fusion(bf16[32,32,896]{2,1,0:T(8,128)(2,1)} %bitcast.11, s32[1024]{0:T(1024)S(1)} %pad_clamp_fusion), kind=kCustom, calls=%fused_computation.6 | custom fusion | bytes 1376304 | tf_op jit(solution)/shard_map/gather | solution.py:224
  60.7 1.2 %collective-permute-start.5 = (bf16[384,896]{1,0:T(8,128)(2,1)}, bf16[384,896]{1,0:T(8,128)(2,1)S(1)}, u32[]{:S(2)}, u32[]{:S(2)}) collective-permute-start(bf16[384,896]{1,0:T(8,128)(2,1)} %bitcast.24), channel_id=1, source_target_pairs={{0,1},{1,0},{2,3},{3,2},{4,5},{5,4},{6,7},{7,6},{8,9},{9,8},{10,11... | collective-permute-start | bytes 2064392 | tf_op jit(solution)/shard_map/ppermute | solution.py:28
  61.9 2.2 %gather_fusion.2 = bf16[12,32,896]{2,1,0:T(8,128)(2,1)S(1)} fusion(bf16[32,32,896]{2,1,0:T(8,128)(2,1)} %bitcast.11, s32[1024]{0:T(1024)S(1)} %pad_clamp_fusion.4), kind=kCustom, calls=%fused_computation.2 | custom fusion | bytes 1376304 | tf_op jit(solution)/shard_map/gather | solution.py:224
  64.1 1.1 %encode.2.refs_0_ = bf16[384,896]{1,0:T(8,128)(2,1)S(1)} custom-call(bf16[384,896]{1,0:T(8,128)(2,1)S(1)} %bitcast.53, bf16[896,896]{1,0:T(8,128)(2,1)S(1)} %bitcast.51), custom_call_target="tpu_custom_call" | custom-call | flops 616562688 | bytes 2981888 | tf_op jit(solution)/shard_map/encode/pallas_call | solution.py:45
  65.2 4.0 %convolution_convert_fusion.1.refs_2_ = bf16[384,2048]{1,0:T(8,128)(2,1)S(1)} fusion(bf16[384,896]{1,0:T(8,128)(2,1)S(1)} %encode.2.refs_0_, bf16[896,2048]{1,0:T(8,128)(2,1)} %refs_4_.1), kind=kOutput, calls=%fused_computation.8 | convolution fusion | flops 1410072576 | bytes 5931008 | tf_op jit(solution)/shard_map/dot_general | solution.py:179
  69.2 7.8 %collective-permute-done.11.refs_7_ = bf16[896,512]{1,0:T(8,128)(2,1)} collective-permute-done((bf16[896,512]{1,0:T(8,128)(2,1)}, bf16[896,512]{1,0:T(8,128)(2,1)}, u32[]{:S(2)}, u32[]{:S(2)}) %collective-permute-start.11) | collective-permute-done | bytes 917536 | tf_op jit(solution)/shard_map/ppermute | solution.py:23
  77.1 0.4 collective-permute-start.13
  77.7 1.8 %convolution_convert_fusion.refs_1_ = bf16[384,2048]{1,0:T(8,128)(2,1)S(1)} fusion(bf16[384,896]{1,0:T(8,128)(2,1)S(1)} %encode.2.refs_0_, bf16[896,2048]{1,0:T(8,128)(2,1)S(1)} %copy-done.1), kind=kOutput, calls=%fused_computation.7 | convolution fusion | flops 1410072576 | bytes 5931008 | tf_op jit(solution)/shard_map/dot_general | solution.py:179
  79.5 1.1 %encode.3.refs_0_.refs_1_ = bf16[384,896]{1,0:T(8,128)(2,1)S(1)} custom-call(bf16[384,896]{1,0:T(8,128)(2,1)S(1)} %collective-permute-done.5.raw_ref, bf16[896,896]{1,0:T(8,128)(2,1)S(1)} %bitcast.52), custom_call_target="tpu_custom_call" | custom-call | flops 616562688 | bytes 2981888 | tf_op jit(solution)/shard_map/encode/pallas_call | solution.py:45
  80.6 0.7 copy-done.3
  81.3 8.9 %attend_own.1.refs_11_ = bf16[352,4096]{1,0:T(8,128)(2,1)} custom-call(s32[2]{0:T(128)S(1)} %pad_add_fusion.info_ref, bf16[384,896]{1,0:T(8,128)(2,1)S(1)} %encode.3.refs_0_.refs_1_, bf16[384,2048]{1,0:T(8,128)(2,1)S(1)} %convolution_convert_fusion.refs_1_, bf16[384,2048]{1,0:T(8,128)(2,1)S(1)} %convolution_convert_fusion.1.refs_2_, ...), custom_call_target="tpu_custom_call" | custom-call | flops 3187671040 | bytes 10911744 | tf_op jit(solution)/shard_map/attend_own/pallas_call | solution.py:138
  90.2 15.0 %attend_sent.1 = bf16[352,4096]{1,0:T(8,128)(2,1)} custom-call(s32[5]{0:T(128)S(1)} %stack.45.info_ref, bf16[384,896]{1,0:T(8,128)(2,1)S(1)} %encode.2.refs_0_, bf16[384,896]{1,0:T(8,128)(2,1)S(1)} %encode.3.refs_0_.refs_1_, bf16[896,512]{1,0:T(8,128)(2,1)} %collective-permute-done.6.refs_2_, ...), custom_call_target="tpu_custom_call", output_to_operand_aliasing={{}: (12, {})} | custom-call | flops 6006243328 | bytes 11599872 | tf_op jit(solution)/shard_map/attend_sent/pallas_call | solution.py:161
  (51 shorter events, 0.7 us)
Async XLA Ops:
  0.0 9.1 %copy-start = (bf16[8,32,896]{2,1,0:T(8,128)(2,1)S(1)}, bf16[8,32,896]{2,1,0:T(8,128)(2,1)}, u32[]{:S(2)}) copy-start(bf16[8,32,896]{2,1,0:T(8,128)(2,1)} %param.8) | copy-start | bytes 1376260
  0.0 11.1 %collective-permute-start.2 = (bf16[56,896]{1,0:T(8,128)(2,1)}, bf16[56,896]{1,0:T(8,128)(2,1)S(1)}, u32[]{:S(2)}, u32[]{:S(2)}) collective-permute-start(bf16[56,896]{1,0:T(8,128)(2,1)} %param.9), channel_id=1, source_target_pairs={{0,24},{2,26},{4,28},{6,30},{8,16},{10,18},{12,20},{14,22},{16,8},... | collective-permute-start | bytes 301064 | tf_op jit(solution)/shard_map/ppermute | solution.py:23
  3.3 8.2 %collective-permute-start = (bf16[56,896]{1,0:T(8,128)(2,1)}, bf16[56,896]{1,0:T(8,128)(2,1)S(1)}, u32[]{:S(2)}, u32[]{:S(2)}) collective-permute-start(bf16[56,896]{1,0:T(8,128)(2,1)} %param.9), channel_id=1, source_target_pairs={{0,16},{2,18},{4,20},{6,22},{8,24},{10,26},{12,28},{14,30},{16,0},... | collective-permute-start | bytes 301064 | tf_op jit(solution)/shard_map/ppermute | solution.py:23
  3.3 8.2 %collective-permute-start.1 = (bf16[56,896]{1,0:T(8,128)(2,1)}, bf16[56,896]{1,0:T(8,128)(2,1)S(1)}, u32[]{:S(2)}, u32[]{:S(2)}) collective-permute-start(bf16[56,896]{1,0:T(8,128)(2,1)} %param.9), channel_id=1, source_target_pairs={{0,8},{2,10},{4,12},{6,14},{8,0},{10,2},{12,4},{14,6},{16,24},{18,... | collective-permute-start | bytes 301064 | tf_op jit(solution)/shard_map/ppermute | solution.py:23
  3.7 4.1 %copy-start.6 = (s32[176,2]{0,1:T(2,128)S(1)}, s32[176,2]{0,1:T(2,128)}, u32[]{:S(2)}) copy-start(s32[176,2]{0,1:T(2,128)} %param.12) | copy-start | bytes 4228
  4.9 42.7 %collective-permute-start.10 = (bf16[896,512]{1,0:T(8,128)(2,1)S(1)}, bf16[896,512]{1,0:T(8,128)(2,1)}, u32[]{:S(2)}, u32[]{:S(2)}) collective-permute-start(bf16[896,512]{1,0:T(8,128)(2,1)S(1)} %constant_dynamic-slice_fusion), channel_id=1, source_target_pairs={{0,1},{1,0},{2,3},{3,2},{4,5},{5,4},{6,7},{7,6},{8,9},{9,8},{10,11... | collective-permute-start | bytes 2752520 | tf_op jit(solution)/shard_map/ppermute | solution.py:28
  7.5 40.2 %collective-permute-start.6 = (bf16[896,512]{1,0:T(8,128)(2,1)S(1)}, bf16[896,512]{1,0:T(8,128)(2,1)}, u32[]{:S(2)}, u32[]{:S(2)}) collective-permute-start(bf16[896,512]{1,0:T(8,128)(2,1)S(1)} %constant_dynamic-slice_fusion.1), channel_id=1, source_target_pairs={{0,1},{1,0},{2,3},{3,2},{4,5},{5,4},{6,7},{7,6},{8,9},{9,8},{10,11... | collective-permute-start | bytes 2752520 | tf_op jit(solution)/shard_map/ppermute | solution.py:28
  9.1 2.5 %copy-start.5 = (bf16[56,896]{1,0:T(8,128)(2,1)S(1)}, bf16[56,896]{1,0:T(8,128)(2,1)}, u32[]{:S(2)}) copy-start(bf16[56,896]{1,0:T(8,128)(2,1)} %param.9) | copy-start | bytes 301060
  11.6 46.0 %all-to-all-start = ((bf16[16,2,32,896]{3,2,1,0:T(8,128)(2,1)}), bf16[16,2,32,896]{3,2,1,0:T(8,128)(2,1)}, u32[]{:S(2)}, u32[]{:S(2)}) async-start(bf16[16,2,32,896]{3,2,1,0:T(8,128)(2,1)} %bitcast.6), calls=%async_computation | async-start | bytes 3670016 | tf_op jit(solution)/shard_map/all_to_all | solution.py:213
  20.2 26.8 %copy-start.4 = (s32[16]{0:T(128)S(1)}, s32[16]{0:T(128)}, u32[]{:S(2)}) copy-start(s32[16]{0:T(128)} %constant.119.clone) | copy-start | bytes 196
  20.9 23.3 %collective-permute-start.3 = (bf16[4,56,896]{2,1,0:T(8,128)(2,1)S(1)}, bf16[4,56,896]{2,1,0:T(8,128)(2,1)S(1)}, u32[]{:S(2)}, u32[]{:S(2)}) collective-permute-start(bf16[4,56,896]{2,1,0:T(8,128)(2,1)S(1)} %pad_maximum_fusion), channel_id=1, source_target_pairs={{0,4},{2,6},{4,0},{6,2},{8,12},{10,14},{12,8},{14,10},{16,20},{18,... | collective-permute-start | bytes 1204232 | tf_op jit(solution)/shard_map/ppermute | solution.py:23
  45.2 3.8 %collective-permute-start.4 = (bf16[8,56,896]{2,1,0:T(8,128)(2,1)}, bf16[8,56,896]{2,1,0:T(8,128)(2,1)S(1)}, u32[]{:S(2)}, u32[]{:S(2)}) collective-permute-start(bf16[8,56,896]{2,1,0:T(8,128)(2,1)} %get-tuple-element.13), channel_id=1, source_target_pairs={{0,2},{2,0},{4,6},{6,4},{8,10},{10,8},{12,14},{14,12},{16,18},{18,... | collective-permute-start | bytes 2408456 | tf_op jit(solution)/shard_map/ppermute | solution.py:23
  47.6 29.4 %collective-permute-start.11 = (bf16[896,512]{1,0:T(8,128)(2,1)}, bf16[896,512]{1,0:T(8,128)(2,1)}, u32[]{:S(2)}, u32[]{:S(2)}) collective-permute-start(bf16[896,512]{1,0:T(8,128)(2,1)} %collective-permute-done.10.refs_6_), channel_id=1, source_target_pairs={{0,8},{2,10},{4,12},{6,14},{8,0},{10,2},{12,4},{14,6},{16,24},{18,... | collective-permute-start | bytes 2752520 | tf_op jit(solution)/shard_map/ppermute | solution.py:23
  47.7 29.8 %collective-permute-start.7 = (bf16[896,512]{1,0:T(8,128)(2,1)}, bf16[896,512]{1,0:T(8,128)(2,1)}, u32[]{:S(2)}, u32[]{:S(2)}) collective-permute-start(bf16[896,512]{1,0:T(8,128)(2,1)} %collective-permute-done.6.refs_2_), channel_id=1, source_target_pairs={{0,4},{2,6},{4,0},{6,2},{8,12},{10,14},{12,8},{14,10},{16,20},{18,... | collective-permute-start | bytes 2752520 | tf_op jit(solution)/shard_map/ppermute | solution.py:23
  48.4 41.8 %collective-permute-start.12 = (bf16[896,512]{1,0:T(8,128)(2,1)}, bf16[896,512]{1,0:T(8,128)(2,1)}, u32[]{:S(2)}, u32[]{:S(2)}) collective-permute-start(bf16[896,512]{1,0:T(8,128)(2,1)} %collective-permute-done.10.refs_6_), channel_id=1, source_target_pairs={{0,2},{2,0},{4,6},{6,4},{8,10},{10,8},{12,14},{14,12},{16,18},{18,... | collective-permute-start | bytes 2752520 | tf_op jit(solution)/shard_map/ppermute | solution.py:23
  48.8 41.4 %collective-permute-start.8 = (bf16[896,512]{1,0:T(8,128)(2,1)}, bf16[896,512]{1,0:T(8,128)(2,1)}, u32[]{:S(2)}, u32[]{:S(2)}) collective-permute-start(bf16[896,512]{1,0:T(8,128)(2,1)} %collective-permute-done.6.refs_2_), channel_id=1, source_target_pairs={{0,2},{2,0},{4,6},{6,4},{8,10},{10,8},{12,14},{14,12},{16,18},{18,... | collective-permute-start | bytes 2752520 | tf_op jit(solution)/shard_map/ppermute | solution.py:23
  60.7 18.8 %collective-permute-start.5 = (bf16[384,896]{1,0:T(8,128)(2,1)}, bf16[384,896]{1,0:T(8,128)(2,1)S(1)}, u32[]{:S(2)}, u32[]{:S(2)}) collective-permute-start(bf16[384,896]{1,0:T(8,128)(2,1)} %bitcast.24), channel_id=1, source_target_pairs={{0,1},{1,0},{2,3},{3,2},{4,5},{5,4},{6,7},{7,6},{8,9},{9,8},{10,11... | collective-permute-start | bytes 2064392 | tf_op jit(solution)/shard_map/ppermute | solution.py:28
  65.2 12.4 %copy-start.1 = (bf16[896,2048]{1,0:T(8,128)(2,1)S(1)}, bf16[896,2048]{1,0:T(8,128)(2,1)}, u32[]{:S(2)}) copy-start(bf16[896,2048]{1,0:T(8,128)(2,1)} %refs_3_.1) | copy-start | bytes 11010052
  77.1 13.2 %collective-permute-start.13 = (bf16[896,512]{1,0:T(8,128)(2,1)}, bf16[896,512]{1,0:T(8,128)(2,1)S(1)}, u32[]{:S(2)}, u32[]{:S(2)}) collective-permute-start(bf16[896,512]{1,0:T(8,128)(2,1)} %collective-permute-done.11.refs_7_), channel_id=1, source_target_pairs={{0,2},{2,0},{4,6},{6,4},{8,10},{10,8},{12,14},{14,12},{16,18},{18,... | collective-permute-start | bytes 2752520 | tf_op jit(solution)/shard_map/ppermute | solution.py:23
  77.5 12.7 %collective-permute-start.9 = (bf16[896,512]{1,0:T(8,128)(2,1)}, bf16[896,512]{1,0:T(8,128)(2,1)S(1)}, u32[]{:S(2)}, u32[]{:S(2)}) collective-permute-start(bf16[896,512]{1,0:T(8,128)(2,1)} %collective-permute-done.7.refs_3_), channel_id=1, source_target_pairs={{0,2},{2,0},{4,6},{6,4},{8,10},{10,8},{12,14},{14,12},{16,18},{18,... | collective-permute-start | bytes 2752520 | tf_op jit(solution)/shard_map/ppermute | solution.py:23
  77.7 3.0 %copy-start.2 = (bf16[896,2048]{1,0:T(8,128)(2,1)S(1)}, bf16[896,2048]{1,0:T(8,128)(2,1)}, u32[]{:S(2)}) copy-start(bf16[896,2048]{1,0:T(8,128)(2,1)} %refs_4_.1) | copy-start | bytes 11010052
  79.5 1.9 %copy-start.3 = (bf16[352,4096]{1,0:T(8,128)(2,1)S(1)}, bf16[352,4096]{1,0:T(8,128)(2,1)}, u32[]{:S(2)}) copy-start(bf16[352,4096]{1,0:T(8,128)(2,1)} %refs_10_.1) | copy-start | bytes 8650756

commit v3 on v2

--- a/solution.py
+++ b/solution.py
@@ -102,16 +102,29 @@
 
 def sent_kernel(parts, info_ref, *refs):
     enc_refs, wk_refs, wv_refs = refs[:parts], refs[parts:parts + SHARERS], refs[parts + SHARERS:parts + 2 * SHARERS]
-    q_ref, _, o_ref, ks_ref, vs_ref, qf_ref, of_ref = refs[parts + 2 * SHARERS:]
+    q_ref, _, o_ref, w_ref, sems, ks_ref, vs_ref, qf_ref, of_ref = refs[parts + 2 * SHARERS:]
+    step = pl.program_id(0)
+    slot = lax.rem(step, 2)
+
+    def fetch(piece, into):
+        return [
+            pltpu.make_async_copy(source, w_ref.at[into, at], sems.at[into, at])
+            for at, source in enumerate((wk_refs[piece], wv_refs[piece]))
+        ]
+
     for piece in range(SHARERS):
-        @pl.when(pl.program_id(0) == piece)
+        @pl.when(step == max(piece - 1, 0))
         def _(piece=piece):
-            k_refs = make_parts(enc_refs, wk_refs[piece][...], ks_ref)
-            v_refs = make_parts(enc_refs, wv_refs[piece][...], vs_ref)
-            attend_heads(
-                functools.partial(span_rows, k_refs), functools.partial(span_rows, v_refs),
-                q_ref, o_ref, qf_ref, of_ref, pl.multiple_of(info_ref[0], 16),
-            )
+            for copy in fetch(piece, piece % 2):
+                copy.start()
+    for copy in fetch(0, slot):
+        copy.wait()
+    k_refs = make_parts(enc_refs, w_ref[slot, 0], ks_ref)
+    v_refs = make_parts(enc_refs, w_ref[slot, 1], vs_ref)
+    attend_heads(
+        functools.partial(span_rows, k_refs), functools.partial(span_rows, v_refs),
+        q_ref, o_ref, qf_ref, of_ref, pl.multiple_of(info_ref[0], 16),
+    )
 
 
 def cost(encoded, rows, columns):
@@ -156,7 +169,7 @@
     part_rows, enc_width = encoded[0].shape
     wide = key_pieces[0].shape[1]
     whole = pl.BlockSpec((part_rows, enc_width), lambda i, s: (0, 0))
-    weights = pl.BlockSpec((enc_width, wide), lambda i, s: (0, 0))
+    weights = pl.BlockSpec(memory_space=pl.ANY)
     block = pl.BlockSpec((rows, wide), lambda i, s: (0, s[1 + i]))
     return pl.pallas_call(
         functools.partial(sent_kernel, parts),
@@ -165,7 +178,10 @@
             grid=(SHARERS,),
             in_specs=[whole] * parts + [weights] * (2 * SHARERS) + [block, pl.BlockSpec(memory_space=pl.ANY)],
             out_specs=block,
-            scratch_shapes=scratch(parts, part_rows, spans, wide),
+            scratch_shapes=[
+                pltpu.VMEM((2, 2, enc_width, wide), jnp.bfloat16), pltpu.SemaphoreType.DMA((2, 2)),
+                *scratch(parts, part_rows, spans, wide),
+            ],
         ),
         out_shape=jax.ShapeDtypeStruct(out.shape, out.dtype),
         input_output_aliases={parts + 2 * SHARERS + 2: 0},

time: 107 us -> 106 us (level)
  no operation moved by 1% of the time
where the time goes in v3:
time: 106 us; the launch traced here: 104 us
  waiting for transfers between devices  34.9 us (33%)
  Pallas kernels  25.2 us (24%)
  local copies, waits for them, and re-layouts  20.1 us (19%)
  starting transfers between devices  17 us (16%)
  matrix products  5.77 us (5%)
    ppermute x11, waiting for transfers between devices, xor_permute(): return lax.ppermute(x, 'seq', [(i, i ^ bits) for i in range(count)])  29.4 us
    pallas_call x1, Pallas kernels, attend_sent(): pl.pallas_call(functools.partial(sent_kernel, parts), grid_spec=pltpu.Pre...  14.1 us
    pallas_call x1, Pallas kernels, attend_own(): pl.pallas_call(functools.partial(own_kernel, len(encoded) + 1), grid_spec...  8.88 us
    all_to_all x1, starting transfers between devices, per_device(): lax.all_to_all(entries, 'seq', split_axis=0, concat_axis=0, tiled=True)  7.52 us
    ppermute x11, starting transfers between devices, xor_permute(): return lax.ppermute(x, 'seq', [(i, i ^ bits) for i in range(count)])  6.62 us
    gather x4, local copies, waits for them, and re-layouts, neighbours_of(): return flat_arrived[cited_slot[places]].reshape(-1, flat_arrived.shape[2])  6.47 us
    dot_general x2, matrix products, project(): jnp.dot(rows, weights, preferred_element_type=jnp.float32)  5.77 us
    all_to_all x1, waiting for transfers between devices, per_device(): lax.all_to_all(entries, 'seq', split_axis=0, concat_axis=0, tiled=True)  5.45 us
  transfers between devices with their start and end apart: 15, of which 4 were waited for; matrix products, arithmetic and copies ran while one was open for 25% of the time, Pallas kernels for 11%

profile of v3, /device:TPU:3, one launch (start us, length us, event | category | flops | bytes accessed | tf_op | source)
XLA Modules:
  0.0 104.3 jit_solution(8431631947591430784)
XLA Ops:
  0.0 3.3 %collective-permute-start.2 = (bf16[56,896]{1,0:T(8,128)(2,1)}, bf16[56,896]{1,0:T(8,128)(2,1)S(1)}, u32[]{:S(2)}, u32[]{:S(2)}) collective-permute-start(bf16[56,896]{1,0:T(8,128)(2,1)} %param.9), channel_id=1, source_target_pairs={{0,24},{2,26},{4,28},{6,30},{8,16},{10,18},{12,20},{14,22},{16,8},... | collective-permute-start | bytes 301064 | tf_op jit(solution)/shard_map/ppermute | solution.py:23
  3.3 0.4 collective-permute-start.1
  3.7 1.3 %constant_dynamic-slice_fusion = bf16[896,512]{1,0:T(8,128)(2,1)S(1)} fusion(bf16[896,2048]{1,0:T(8,128)(2,1)} %refs_4_.1, s32[]{:T(128)S(6)} %select_n.156), kind=kLoop, calls=%fused_computation.51 | loop fusion | bytes 1835012 | tf_op jit(solution)/shard_map/dynamic_slice | solution.py:255
  4.9 1.3 %collective-permute-start.10 = (bf16[896,512]{1,0:T(8,128)(2,1)S(1)}, bf16[896,512]{1,0:T(8,128)(2,1)}, u32[]{:S(2)}, u32[]{:S(2)}) collective-permute-start(bf16[896,512]{1,0:T(8,128)(2,1)S(1)} %constant_dynamic-slice_fusion), channel_id=1, source_target_pairs={{0,1},{1,0},{2,3},{3,2},{4,5},{5,4},{6,7},{7,6},{8,9},{9,8},{10,11... | collective-permute-start | bytes 2752520 | tf_op jit(solution)/shard_map/ppermute | solution.py:28
  6.2 1.2 %constant_dynamic-slice_fusion.1 = bf16[896,512]{1,0:T(8,128)(2,1)S(1)} fusion(bf16[896,2048]{1,0:T(8,128)(2,1)} %refs_3_.1, s32[]{:T(128)S(6)} %select_n.156), kind=kLoop, calls=%fused_computation.52 | loop fusion | bytes 1835012 | tf_op jit(solution)/shard_map/dynamic_slice | solution.py:255
  7.5 0.3 collective-permute-start.6
  7.8 0.1 copy.32
  7.9 0.1 reshape.260
  8.1 0.1 copy.33
  8.1 0.5 convert_reduce_fusion
  8.8 0.1 select_reduce_fusion
  8.9 0.1 copy.35
  9.0 0.1 reshape.267
  9.1 2.0 %gather_fusion = bf16[32,32,896]{2,1,0:T(8,128)(2,1)} fusion(bf16[8,32,896]{2,1,0:T(8,128)(2,1)S(1)} %copy-done, s32[1024]{0:T(1024)S(1)} %pad_clamp_fusion.6), kind=kCustom, calls=%fused_computation | custom fusion | bytes 3670144 | tf_op jit(solution)/shard_map/gather | solution.py:228
  11.1 0.5 collective-permute-done
  11.6 7.5 %all-to-all-start = ((bf16[16,2,32,896]{3,2,1,0:T(8,128)(2,1)}), bf16[16,2,32,896]{3,2,1,0:T(8,128)(2,1)}, u32[]{:S(2)}, u32[]{:S(2)}) async-start(bf16[16,2,32,896]{3,2,1,0:T(8,128)(2,1)} %bitcast.6), calls=%async_computation | async-start | bytes 3670016 | tf_op jit(solution)/shard_map/all_to_all | solution.py:229
  19.2 0.1 add.242
  19.4 0.1 add.230
  19.5 0.7 gather_fusion.5
  20.2 0.7 constant_dynamic-update-slice_fusion.4
  20.9 0.1 collective-permute-start.3
  21.0 0.7 constant_dynamic-update-slice_fusion.3
  21.7 0.7 constant_dynamic-update-slice_fusion.2
  22.4 0.7 constant_dynamic-update-slice_fusion.1
  23.1 21.1 %collective-permute-done.3 = bf16[4,56,896]{2,1,0:T(8,128)(2,1)S(1)} collective-permute-done((bf16[4,56,896]{2,1,0:T(8,128)(2,1)S(1)}, bf16[4,56,896]{2,1,0:T(8,128)(2,1)S(1)}, u32[]{:S(2)}, u32[]{:S(2)}) %collective-permute-start.3) | collective-permute-done | bytes 401440 | tf_op jit(solution)/shard_map/ppermute | solution.py:23
  44.2 1.0 constant_dynamic-update-slice_fusion
  45.2 1.1 %collective-permute-start.4 = (bf16[8,56,896]{2,1,0:T(8,128)(2,1)}, bf16[8,56,896]{2,1,0:T(8,128)(2,1)S(1)}, u32[]{:S(2)}, u32[]{:S(2)}) collective-permute-start(bf16[8,56,896]{2,1,0:T(8,128)(2,1)} %get-tuple-element.13), channel_id=1, source_target_pairs={{0,2},{2,0},{4,6},{6,4},{8,10},{10,8},{12,14},{14,12},{16,18},{18,... | collective-permute-start | bytes 2408456 | tf_op jit(solution)/shard_map/ppermute | solution.py:23
  46.3 0.7 gather_fusion.1
  47.0 0.7 gather_fusion.3
  47.7 0.6 collective-permute-start.7
  48.3 0.1 stack.45.info_ref
  48.4 0.4 collective-permute-start.12
  48.8 0.2 collective-permute-start.8
  49.0 1.0 constant_dynamic-update-slice_fusion.5
  50.0 2.2 %gather_fusion.4 = bf16[16,56,896]{2,1,0:T(8,128)(2,1)S(1)} fusion(bf16[16,56,896]{2,1,0:T(8,128)(2,1)} %constant_dynamic-update-slice_fusion.5, s32[1024]{0:T(1024)S(1)} %pad_clamp_fusion.2), kind=kCustom, calls=%fused_computation.4 | custom fusion | bytes 3211328 | tf_op jit(solution)/shard_map/gather | solution.py:213
  52.2 5.4 %all-to-all-done = bf16[16,2,32,896]{3,2,1,0:T(8,128)(2,1)} async-done(((bf16[16,2,32,896]{3,2,1,0:T(8,128)(2,1)}), bf16[16,2,32,896]{3,2,1,0:T(8,128)(2,1)}, u32[]{:S(2)}, u32[]{:S(2)}) %all-to-all-start) | async-done | bytes 1835040 | tf_op jit(solution)/shard_map/all_to_all | solution.py:229
  57.7 3.0 %gather_fusion.6 = bf16[12,32,896]{2,1,0:T(8,128)(2,1)} fusion(bf16[32,32,896]{2,1,0:T(8,128)(2,1)} %bitcast.11, s32[1024]{0:T(1024)S(1)} %pad_clamp_fusion), kind=kCustom, calls=%fused_computation.6 | custom fusion | bytes 1376304 | tf_op jit(solution)/shard_map/gather | solution.py:240
  60.7 1.2 %collective-permute-start.5 = (bf16[384,896]{1,0:T(8,128)(2,1)}, bf16[384,896]{1,0:T(8,128)(2,1)S(1)}, u32[]{:S(2)}, u32[]{:S(2)}) collective-permute-start(bf16[384,896]{1,0:T(8,128)(2,1)} %bitcast.24), channel_id=1, source_target_pairs={{0,1},{1,0},{2,3},{3,2},{4,5},{5,4},{6,7},{7,6},{8,9},{9,8},{10,11... | collective-permute-start | bytes 2064392 | tf_op jit(solution)/shard_map/ppermute | solution.py:28
  61.9 2.2 %gather_fusion.2 = bf16[12,32,896]{2,1,0:T(8,128)(2,1)S(1)} fusion(bf16[32,32,896]{2,1,0:T(8,128)(2,1)} %bitcast.11, s32[1024]{0:T(1024)S(1)} %pad_clamp_fusion.4), kind=kCustom, calls=%fused_computation.2 | custom fusion | bytes 1376304 | tf_op jit(solution)/shard_map/gather | solution.py:240
  64.1 1.1 %encode.2.refs_0_ = bf16[384,896]{1,0:T(8,128)(2,1)S(1)} custom-call(bf16[384,896]{1,0:T(8,128)(2,1)S(1)} %bitcast.53, bf16[896,896]{1,0:T(8,128)(2,1)S(1)} %bitcast.51), custom_call_target="tpu_custom_call" | custom-call | flops 616562688 | bytes 2981888 | tf_op jit(solution)/shard_map/encode/pallas_call | solution.py:45
  65.2 4.0 %convolution_convert_fusion.1.refs_2_ = bf16[384,2048]{1,0:T(8,128)(2,1)S(1)} fusion(bf16[384,896]{1,0:T(8,128)(2,1)S(1)} %encode.2.refs_0_, bf16[896,2048]{1,0:T(8,128)(2,1)} %refs_4_.1), kind=kOutput, calls=%fused_computation.8 | convolution fusion | flops 1410072576 | bytes 5931008 | tf_op jit(solution)/shard_map/dot_general | solution.py:195
  69.2 7.8 %collective-permute-done.11.refs_7_ = bf16[896,512]{1,0:T(8,128)(2,1)} collective-permute-done((bf16[896,512]{1,0:T(8,128)(2,1)}, bf16[896,512]{1,0:T(8,128)(2,1)}, u32[]{:S(2)}, u32[]{:S(2)}) %collective-permute-start.11) | collective-permute-done | bytes 917536 | tf_op jit(solution)/shard_map/ppermute | solution.py:23
  77.1 0.4 collective-permute-start.13
  77.7 1.8 %convolution_convert_fusion.refs_1_ = bf16[384,2048]{1,0:T(8,128)(2,1)S(1)} fusion(bf16[384,896]{1,0:T(8,128)(2,1)S(1)} %encode.2.refs_0_, bf16[896,2048]{1,0:T(8,128)(2,1)S(1)} %copy-done.1), kind=kOutput, calls=%fused_computation.7 | convolution fusion | flops 1410072576 | bytes 5931008 | tf_op jit(solution)/shard_map/dot_general | solution.py:195
  79.5 1.1 %encode.3.refs_0_.refs_1_ = bf16[384,896]{1,0:T(8,128)(2,1)S(1)} custom-call(bf16[384,896]{1,0:T(8,128)(2,1)S(1)} %collective-permute-done.5.raw_ref, bf16[896,896]{1,0:T(8,128)(2,1)S(1)} %bitcast.52), custom_call_target="tpu_custom_call" | custom-call | flops 616562688 | bytes 2981888 | tf_op jit(solution)/shard_map/encode/pallas_call | solution.py:45
  80.6 0.7 copy-done.3
  81.3 8.9 %attend_own.1.refs_11_ = bf16[352,4096]{1,0:T(8,128)(2,1)} custom-call(s32[2]{0:T(128)S(1)} %pad_add_fusion.info_ref, bf16[384,896]{1,0:T(8,128)(2,1)S(1)} %encode.3.refs_0_.refs_1_, bf16[384,2048]{1,0:T(8,128)(2,1)S(1)} %convolution_convert_fusion.refs_1_, bf16[384,2048]{1,0:T(8,128)(2,1)S(1)} %convolution_convert_fusion.1.refs_2_, ...), custom_call_target="tpu_custom_call" | custom-call | flops 3187671040 | bytes 10911744 | tf_op jit(solution)/shard_map/attend_own/pallas_call | solution.py:151
  90.2 14.1 %attend_sent.1 = bf16[352,4096]{1,0:T(8,128)(2,1)} custom-call(s32[5]{0:T(128)S(1)} %stack.45.info_ref, bf16[384,896]{1,0:T(8,128)(2,1)S(1)} %encode.2.refs_0_, bf16[384,896]{1,0:T(8,128)(2,1)S(1)} %encode.3.refs_0_.refs_1_, bf16[896,512]{1,0:T(8,128)(2,1)} %collective-permute-done.6.refs_2_, ...), custom_call_target="tpu_custom_call", output_to_operand_aliasing={{}: (12, {})} | custom-call | flops 6006243328 | bytes 11599872 | tf_op jit(solution)/shard_map/attend_sent/pallas_call | solution.py:174
  (51 shorter events, 0.7 us)
Async XLA Ops:
  0.0 9.1 %copy-start = (bf16[8,32,896]{2,1,0:T(8,128)(2,1)S(1)}, bf16[8,32,896]{2,1,0:T(8,128)(2,1)}, u32[]{:S(2)}) copy-start(bf16[8,32,896]{2,1,0:T(8,128)(2,1)} %param.8) | copy-start | bytes 1376260
  0.0 11.1 %collective-permute-start.2 = (bf16[56,896]{1,0:T(8,128)(2,1)}, bf16[56,896]{1,0:T(8,128)(2,1)S(1)}, u32[]{:S(2)}, u32[]{:S(2)}) collective-permute-start(bf16[56,896]{1,0:T(8,128)(2,1)} %param.9), channel_id=1, source_target_pairs={{0,24},{2,26},{4,28},{6,30},{8,16},{10,18},{12,20},{14,22},{16,8},... | collective-permute-start | bytes 301064 | tf_op jit(solution)/shard_map/ppermute | solution.py:23
  3.3 8.2 %collective-permute-start = (bf16[56,896]{1,0:T(8,128)(2,1)}, bf16[56,896]{1,0:T(8,128)(2,1)S(1)}, u32[]{:S(2)}, u32[]{:S(2)}) collective-permute-start(bf16[56,896]{1,0:T(8,128)(2,1)} %param.9), channel_id=1, source_target_pairs={{0,16},{2,18},{4,20},{6,22},{8,24},{10,26},{12,28},{14,30},{16,0},... | collective-permute-start | bytes 301064 | tf_op jit(solution)/shard_map/ppermute | solution.py:23
  3.3 8.2 %collective-permute-start.1 = (bf16[56,896]{1,0:T(8,128)(2,1)}, bf16[56,896]{1,0:T(8,128)(2,1)S(1)}, u32[]{:S(2)}, u32[]{:S(2)}) collective-permute-start(bf16[56,896]{1,0:T(8,128)(2,1)} %param.9), channel_id=1, source_target_pairs={{0,8},{2,10},{4,12},{6,14},{8,0},{10,2},{12,4},{14,6},{16,24},{18,... | collective-permute-start | bytes 301064 | tf_op jit(solution)/shard_map/ppermute | solution.py:23
  3.7 4.1 %copy-start.6 = (s32[176,2]{0,1:T(2,128)S(1)}, s32[176,2]{0,1:T(2,128)}, u32[]{:S(2)}) copy-start(s32[176,2]{0,1:T(2,128)} %param.12) | copy-start | bytes 4228
  4.9 42.7 %collective-permute-start.10 = (bf16[896,512]{1,0:T(8,128)(2,1)S(1)}, bf16[896,512]{1,0:T(8,128)(2,1)}, u32[]{:S(2)}, u32[]{:S(2)}) collective-permute-start(bf16[896,512]{1,0:T(8,128)(2,1)S(1)} %constant_dynamic-slice_fusion), channel_id=1, source_target_pairs={{0,1},{1,0},{2,3},{3,2},{4,5},{5,4},{6,7},{7,6},{8,9},{9,8},{10,11... | collective-permute-start | bytes 2752520 | tf_op jit(solution)/shard_map/ppermute | solution.py:28
  7.5 40.2 %collective-permute-start.6 = (bf16[896,512]{1,0:T(8,128)(2,1)S(1)}, bf16[896,512]{1,0:T(8,128)(2,1)}, u32[]{:S(2)}, u32[]{:S(2)}) collective-permute-start(bf16[896,512]{1,0:T(8,128)(2,1)S(1)} %constant_dynamic-slice_fusion.1), channel_id=1, source_target_pairs={{0,1},{1,0},{2,3},{3,2},{4,5},{5,4},{6,7},{7,6},{8,9},{9,8},{10,11... | collective-permute-start | bytes 2752520 | tf_op jit(solution)/shard_map/ppermute | solution.py:28
  9.1 2.5 %copy-start.5 = (bf16[56,896]{1,0:T(8,128)(2,1)S(1)}, bf16[56,896]{1,0:T(8,128)(2,1)}, u32[]{:S(2)}) copy-start(bf16[56,896]{1,0:T(8,128)(2,1)} %param.9) | copy-start | bytes 301060
  11.6 46.0 %all-to-all-start = ((bf16[16,2,32,896]{3,2,1,0:T(8,128)(2,1)}), bf16[16,2,32,896]{3,2,1,0:T(8,128)(2,1)}, u32[]{:S(2)}, u32[]{:S(2)}) async-start(bf16[16,2,32,896]{3,2,1,0:T(8,128)(2,1)} %bitcast.6), calls=%async_computation | async-start | bytes 3670016 | tf_op jit(solution)/shard_map/all_to_all | solution.py:229
  20.2 26.8 %copy-start.4 = (s32[16]{0:T(128)S(1)}, s32[16]{0:T(128)}, u32[]{:S(2)}) copy-start(s32[16]{0:T(128)} %constant.119.clone) | copy-start | bytes 196
  20.9 23.3 %collective-permute-start.3 = (bf16[4,56,896]{2,1,0:T(8,128)(2,1)S(1)}, bf16[4,56,896]{2,1,0:T(8,128)(2,1)S(1)}, u32[]{:S(2)}, u32[]{:S(2)}) collective-permute-start(bf16[4,56,896]{2,1,0:T(8,128)(2,1)S(1)} %pad_maximum_fusion), channel_id=1, source_target_pairs={{0,4},{2,6},{4,0},{6,2},{8,12},{10,14},{12,8},{14,10},{16,20},{18,... | collective-permute-start | bytes 1204232 | tf_op jit(solution)/shard_map/ppermute | solution.py:23
  45.2 3.8 %collective-permute-start.4 = (bf16[8,56,896]{2,1,0:T(8,128)(2,1)}, bf16[8,56,896]{2,1,0:T(8,128)(2,1)S(1)}, u32[]{:S(2)}, u32[]{:S(2)}) collective-permute-start(bf16[8,56,896]{2,1,0:T(8,128)(2,1)} %get-tuple-element.13), channel_id=1, source_target_pairs={{0,2},{2,0},{4,6},{6,4},{8,10},{10,8},{12,14},{14,12},{16,18},{18,... | collective-permute-start | bytes 2408456 | tf_op jit(solution)/shard_map/ppermute | solution.py:23
  47.6 29.4 %collective-permute-start.11 = (bf16[896,512]{1,0:T(8,128)(2,1)}, bf16[896,512]{1,0:T(8,128)(2,1)}, u32[]{:S(2)}, u32[]{:S(2)}) collective-permute-start(bf16[896,512]{1,0:T(8,128)(2,1)} %collective-permute-done.10.refs_6_), channel_id=1, source_target_pairs={{0,8},{2,10},{4,12},{6,14},{8,0},{10,2},{12,4},{14,6},{16,24},{18,... | collective-permute-start | bytes 2752520 | tf_op jit(solution)/shard_map/ppermute | solution.py:23
  47.7 29.8 %collective-permute-start.7 = (bf16[896,512]{1,0:T(8,128)(2,1)}, bf16[896,512]{1,0:T(8,128)(2,1)}, u32[]{:S(2)}, u32[]{:S(2)}) collective-permute-start(bf16[896,512]{1,0:T(8,128)(2,1)} %collective-permute-done.6.refs_2_), channel_id=1, source_target_pairs={{0,4},{2,6},{4,0},{6,2},{8,12},{10,14},{12,8},{14,10},{16,20},{18,... | collective-permute-start | bytes 2752520 | tf_op jit(solution)/shard_map/ppermute | solution.py:23
  48.4 41.8 %collective-permute-start.12 = (bf16[896,512]{1,0:T(8,128)(2,1)}, bf16[896,512]{1,0:T(8,128)(2,1)}, u32[]{:S(2)}, u32[]{:S(2)}) collective-permute-start(bf16[896,512]{1,0:T(8,128)(2,1)} %collective-permute-done.10.refs_6_), channel_id=1, source_target_pairs={{0,2},{2,0},{4,6},{6,4},{8,10},{10,8},{12,14},{14,12},{16,18},{18,... | collective-permute-start | bytes 2752520 | tf_op jit(solution)/shard_map/ppermute | solution.py:23
  48.8 41.4 %collective-permute-start.8 = (bf16[896,512]{1,0:T(8,128)(2,1)}, bf16[896,512]{1,0:T(8,128)(2,1)}, u32[]{:S(2)}, u32[]{:S(2)}) collective-permute-start(bf16[896,512]{1,0:T(8,128)(2,1)} %collective-permute-done.6.refs_2_), channel_id=1, source_target_pairs={{0,2},{2,0},{4,6},{6,4},{8,10},{10,8},{12,14},{14,12},{16,18},{18,... | collective-permute-start | bytes 2752520 | tf_op jit(solution)/shard_map/ppermute | solution.py:23
  60.7 18.8 %collective-permute-start.5 = (bf16[384,896]{1,0:T(8,128)(2,1)}, bf16[384,896]{1,0:T(8,128)(2,1)S(1)}, u32[]{:S(2)}, u32[]{:S(2)}) collective-permute-start(bf16[384,896]{1,0:T(8,128)(2,1)} %bitcast.24), channel_id=1, source_target_pairs={{0,1},{1,0},{2,3},{3,2},{4,5},{5,4},{6,7},{7,6},{8,9},{9,8},{10,11... | collective-permute-start | bytes 2064392 | tf_op jit(solution)/shard_map/ppermute | solution.py:28
  65.2 12.4 %copy-start.1 = (bf16[896,2048]{1,0:T(8,128)(2,1)S(1)}, bf16[896,2048]{1,0:T(8,128)(2,1)}, u32[]{:S(2)}) copy-start(bf16[896,2048]{1,0:T(8,128)(2,1)} %refs_3_.1) | copy-start | bytes 11010052
  77.1 13.2 %collective-permute-start.13 = (bf16[896,512]{1,0:T(8,128)(2,1)}, bf16[896,512]{1,0:T(8,128)(2,1)S(1)}, u32[]{:S(2)}, u32[]{:S(2)}) collective-permute-start(bf16[896,512]{1,0:T(8,128)(2,1)} %collective-permute-done.11.refs_7_), channel_id=1, source_target_pairs={{0,2},{2,0},{4,6},{6,4},{8,10},{10,8},{12,14},{14,12},{16,18},{18,... | collective-permute-start | bytes 2752520 | tf_op jit(solution)/shard_map/ppermute | solution.py:23
  77.5 12.7 %collective-permute-start.9 = (bf16[896,512]{1,0:T(8,128)(2,1)}, bf16[896,512]{1,0:T(8,128)(2,1)S(1)}, u32[]{:S(2)}, u32[]{:S(2)}) collective-permute-start(bf16[896,512]{1,0:T(8,128)(2,1)} %collective-permute-done.7.refs_3_), channel_id=1, source_target_pairs={{0,2},{2,0},{4,6},{6,4},{8,10},{10,8},{12,14},{14,12},{16,18},{18,... | collective-permute-start | bytes 2752520 | tf_op jit(solution)/shard_map/ppermute | solution.py:23
  77.7 3.0 %copy-start.2 = (bf16[896,2048]{1,0:T(8,128)(2,1)S(1)}, bf16[896,2048]{1,0:T(8,128)(2,1)}, u32[]{:S(2)}) copy-start(bf16[896,2048]{1,0:T(8,128)(2,1)} %refs_4_.1) | copy-start | bytes 11010052
  79.5 1.9 %copy-start.3 = (bf16[352,4096]{1,0:T(8,128)(2,1)S(1)}, bf16[352,4096]{1,0:T(8,128)(2,1)}, u32[]{:S(2)}) copy-start(bf16[352,4096]{1,0:T(8,128)(2,1)} %refs_10_.1) | copy-start | bytes 8650756

commit v4 on v3

--- a/solution.py
+++ b/solution.py
@@ -251,7 +251,7 @@
     sent = []
     for shift in range(1, head_count):
         shared = []
-        for weights, axis_bit in ((w_key, 2), (w_value, 4)):
+        for weights, axis_bit in ((w_key, 4), (w_value, 2)):
             first = shift_heads(lax.dynamic_slice_in_dim(weights, piece_index * piece_cols, piece_cols, 1), shift)
             second = xor_permute(first, axis_bit)
             shared.append((first, second, xor_permute(first, 1), xor_permute(after(second, own_values), 1)))

time: 106 us -> 106 us (level)
  transfers between devices with their start and end apart: 15 -> 15, of which waited for: 4 -> 5; matrix products, arithmetic and copies ran while one was open for 25% -> 25% of each run, Pallas kernels for 11% -> 11%
where the time goes in v4:
time: 106 us; the launch traced here: 104 us
  waiting for transfers between devices  34 us (32%)
  Pallas kernels  25.2 us (24%)
  local copies, waits for them, and re-layouts  20.1 us (19%)
  starting transfers between devices  17.7 us (17%)
  matrix products  5.77 us (5%)
    ppermute x11, waiting for transfers between devices, xor_permute(): return lax.ppermute(x, 'seq', [(i, i ^ bits) for i in range(count)])  28.7 us
    pallas_call x1, Pallas kernels, attend_sent(): pl.pallas_call(functools.partial(sent_kernel, parts), grid_spec=pltpu.Pre...  14.1 us
    pallas_call x1, Pallas kernels, attend_own(): pl.pallas_call(functools.partial(own_kernel, len(encoded) + 1), grid_spec...  8.88 us
    all_to_all x1, starting transfers between devices, per_device(): lax.all_to_all(entries, 'seq', split_axis=0, concat_axis=0, tiled=True)  7.52 us
    ppermute x11, starting transfers between devices, xor_permute(): return lax.ppermute(x, 'seq', [(i, i ^ bits) for i in range(count)])  7.38 us
    gather x4, local copies, waits for them, and re-layouts, neighbours_of(): return flat_arrived[cited_slot[places]].reshape(-1, flat_arrived.shape[2])  6.47 us
    dot_general x2, matrix products, project(): jnp.dot(rows, weights, preferred_element_type=jnp.float32)  5.77 us
    all_to_all x1, waiting for transfers between devices, per_device(): lax.all_to_all(entries, 'seq', split_axis=0, concat_axis=0, tiled=True)  5.26 us
  transfers between devices with their start and end apart: 15, of which 5 were waited for; matrix products, arithmetic and copies ran while one was open for 25% of the time, Pallas kernels for 11%

profile of v4, /device:TPU:3, one launch (start us, length us, event | category | flops | bytes accessed | tf_op | source)
XLA Modules:
  0.0 104.2 jit_solution(12496209707017130463)
XLA Ops:
  0.0 3.3 %collective-permute-start.2 = (bf16[56,896]{1,0:T(8,128)(2,1)}, bf16[56,896]{1,0:T(8,128)(2,1)S(1)}, u32[]{:S(2)}, u32[]{:S(2)}) collective-permute-start(bf16[56,896]{1,0:T(8,128)(2,1)} %param.9), channel_id=1, source_target_pairs={{0,24},{2,26},{4,28},{6,30},{8,16},{10,18},{12,20},{14,22},{16,8},... | collective-permute-start | bytes 301064 | tf_op jit(solution)/shard_map/ppermute | solution.py:23
  3.3 0.4 collective-permute-start.1
  3.7 1.3 %constant_dynamic-slice_fusion = bf16[896,512]{1,0:T(8,128)(2,1)S(1)} fusion(bf16[896,2048]{1,0:T(8,128)(2,1)} %refs_4_.1, s32[]{:T(128)S(6)} %select_n.156), kind=kLoop, calls=%fused_computation.51 | loop fusion | bytes 1835012 | tf_op jit(solution)/shard_map/dynamic_slice | solution.py:255
  4.9 1.3 %collective-permute-start.10 = (bf16[896,512]{1,0:T(8,128)(2,1)S(1)}, bf16[896,512]{1,0:T(8,128)(2,1)}, u32[]{:S(2)}, u32[]{:S(2)}) collective-permute-start(bf16[896,512]{1,0:T(8,128)(2,1)S(1)} %constant_dynamic-slice_fusion), channel_id=1, source_target_pairs={{0,1},{1,0},{2,3},{3,2},{4,5},{5,4},{6,7},{7,6},{8,9},{9,8},{10,11... | collective-permute-start | bytes 2752520 | tf_op jit(solution)/shard_map/ppermute | solution.py:28
  6.2 1.2 %constant_dynamic-slice_fusion.1 = bf16[896,512]{1,0:T(8,128)(2,1)S(1)} fusion(bf16[896,2048]{1,0:T(8,128)(2,1)} %refs_3_.1, s32[]{:T(128)S(6)} %select_n.156), kind=kLoop, calls=%fused_computation.52 | loop fusion | bytes 1835012 | tf_op jit(solution)/shard_map/dynamic_slice | solution.py:255
  7.5 0.3 collective-permute-start.6
  7.8 0.1 copy.32
  7.9 0.1 reshape.260
  8.1 0.1 copy.33
  8.1 0.5 convert_reduce_fusion
  8.8 0.1 select_reduce_fusion
  8.9 0.1 copy.35
  9.0 0.1 reshape.267
  9.1 2.0 %gather_fusion = bf16[32,32,896]{2,1,0:T(8,128)(2,1)} fusion(bf16[8,32,896]{2,1,0:T(8,128)(2,1)S(1)} %copy-done, s32[1024]{0:T(1024)S(1)} %pad_clamp_fusion.6), kind=kCustom, calls=%fused_computation | custom fusion | bytes 3670144 | tf_op jit(solution)/shard_map/gather | solution.py:228
  11.1 0.5 collective-permute-done
  11.6 7.5 %all-to-all-start = ((bf16[16,2,32,896]{3,2,1,0:T(8,128)(2,1)}), bf16[16,2,32,896]{3,2,1,0:T(8,128)(2,1)}, u32[]{:S(2)}, u32[]{:S(2)}) async-start(bf16[16,2,32,896]{3,2,1,0:T(8,128)(2,1)} %bitcast.6), calls=%async_computation | async-start | bytes 3670016 | tf_op jit(solution)/shard_map/all_to_all | solution.py:229
  19.2 0.1 add.242
  19.4 0.1 add.230
  19.5 0.7 gather_fusion.5
  20.2 0.7 constant_dynamic-update-slice_fusion.4
  21.0 0.7 constant_dynamic-update-slice_fusion.3
  21.7 0.7 constant_dynamic-update-slice_fusion.2
  22.4 0.7 constant_dynamic-update-slice_fusion.1
  23.1 21.1 %collective-permute-done.3 = bf16[4,56,896]{2,1,0:T(8,128)(2,1)S(1)} collective-permute-done((bf16[4,56,896]{2,1,0:T(8,128)(2,1)S(1)}, bf16[4,56,896]{2,1,0:T(8,128)(2,1)S(1)}, u32[]{:S(2)}, u32[]{:S(2)}) %collective-permute-start.3) | collective-permute-done | bytes 401440 | tf_op jit(solution)/shard_map/ppermute | solution.py:23
  44.2 1.0 constant_dynamic-update-slice_fusion
  45.2 1.1 %collective-permute-start.4 = (bf16[8,56,896]{2,1,0:T(8,128)(2,1)}, bf16[8,56,896]{2,1,0:T(8,128)(2,1)S(1)}, u32[]{:S(2)}, u32[]{:S(2)}) collective-permute-start(bf16[8,56,896]{2,1,0:T(8,128)(2,1)} %get-tuple-element.13), channel_id=1, source_target_pairs={{0,2},{2,0},{4,6},{6,4},{8,10},{10,8},{12,14},{14,12},{16,18},{18,... | collective-permute-start | bytes 2408456 | tf_op jit(solution)/shard_map/ppermute | solution.py:23
  46.3 0.7 gather_fusion.1
  47.0 0.7 gather_fusion.3
  47.6 0.6 collective-permute-start.11
  48.3 0.1 stack.45.info_ref
  48.4 0.7 collective-permute-start.12
  49.2 1.0 constant_dynamic-update-slice_fusion.5
  50.1 2.2 %gather_fusion.4 = bf16[16,56,896]{2,1,0:T(8,128)(2,1)S(1)} fusion(bf16[16,56,896]{2,1,0:T(8,128)(2,1)} %constant_dynamic-update-slice_fusion.5, s32[1024]{0:T(1024)S(1)} %pad_clamp_fusion.2), kind=kCustom, calls=%fused_computation.4 | custom fusion | bytes 3211328 | tf_op jit(solution)/shard_map/gather | solution.py:213
  52.4 5.3 %all-to-all-done = bf16[16,2,32,896]{3,2,1,0:T(8,128)(2,1)} async-done(((bf16[16,2,32,896]{3,2,1,0:T(8,128)(2,1)}), bf16[16,2,32,896]{3,2,1,0:T(8,128)(2,1)}, u32[]{:S(2)}, u32[]{:S(2)}) %all-to-all-start) | async-done | bytes 1835040 | tf_op jit(solution)/shard_map/all_to_all | solution.py:229
  57.7 3.0 %gather_fusion.6 = bf16[12,32,896]{2,1,0:T(8,128)(2,1)} fusion(bf16[32,32,896]{2,1,0:T(8,128)(2,1)} %bitcast.11, s32[1024]{0:T(1024)S(1)} %pad_clamp_fusion), kind=kCustom, calls=%fused_computation.6 | custom fusion | bytes 1376304 | tf_op jit(solution)/shard_map/gather | solution.py:240
  60.7 1.2 %collective-permute-start.5 = (bf16[384,896]{1,0:T(8,128)(2,1)}, bf16[384,896]{1,0:T(8,128)(2,1)S(1)}, u32[]{:S(2)}, u32[]{:S(2)}) collective-permute-start(bf16[384,896]{1,0:T(8,128)(2,1)} %bitcast.24), channel_id=1, source_target_pairs={{0,1},{1,0},{2,3},{3,2},{4,5},{5,4},{6,7},{7,6},{8,9},{9,8},{10,11... | collective-permute-start | bytes 2064392 | tf_op jit(solution)/shard_map/ppermute | solution.py:28
  61.9 2.2 %gather_fusion.2 = bf16[12,32,896]{2,1,0:T(8,128)(2,1)S(1)} fusion(bf16[32,32,896]{2,1,0:T(8,128)(2,1)} %bitcast.11, s32[1024]{0:T(1024)S(1)} %pad_clamp_fusion.4), kind=kCustom, calls=%fused_computation.2 | custom fusion | bytes 1376304 | tf_op jit(solution)/shard_map/gather | solution.py:240
  64.1 1.1 %encode.2.refs_0_ = bf16[384,896]{1,0:T(8,128)(2,1)S(1)} custom-call(bf16[384,896]{1,0:T(8,128)(2,1)S(1)} %bitcast.53, bf16[896,896]{1,0:T(8,128)(2,1)S(1)} %bitcast.51), custom_call_target="tpu_custom_call" | custom-call | flops 616562688 | bytes 2981888 | tf_op jit(solution)/shard_map/encode/pallas_call | solution.py:45
  65.2 4.0 %convolution_convert_fusion.1.refs_2_ = bf16[384,2048]{1,0:T(8,128)(2,1)S(1)} fusion(bf16[384,896]{1,0:T(8,128)(2,1)S(1)} %encode.2.refs_0_, bf16[896,2048]{1,0:T(8,128)(2,1)} %refs_4_.1), kind=kOutput, calls=%fused_computation.8 | convolution fusion | flops 1410072576 | bytes 5931008 | tf_op jit(solution)/shard_map/dot_general | solution.py:195
  69.2 3.9 %collective-permute-done.11.refs_7_ = bf16[896,512]{1,0:T(8,128)(2,1)} collective-permute-done((bf16[896,512]{1,0:T(8,128)(2,1)}, bf16[896,512]{1,0:T(8,128)(2,1)}, u32[]{:S(2)}, u32[]{:S(2)}) %collective-permute-start.11) | collective-permute-done | bytes 917536 | tf_op jit(solution)/shard_map/ppermute | solution.py:23
  73.2 0.6 collective-permute-start.13
  73.8 3.2 %collective-permute-done.7.refs_3_ = bf16[896,512]{1,0:T(8,128)(2,1)} collective-permute-done((bf16[896,512]{1,0:T(8,128)(2,1)}, bf16[896,512]{1,0:T(8,128)(2,1)}, u32[]{:S(2)}, u32[]{:S(2)}) %collective-permute-start.7) | collective-permute-done | bytes 917536 | tf_op jit(solution)/shard_map/ppermute | solution.py:23
  77.0 0.5 collective-permute-start.9
  77.6 1.8 %convolution_convert_fusion.refs_1_ = bf16[384,2048]{1,0:T(8,128)(2,1)S(1)} fusion(bf16[384,896]{1,0:T(8,128)(2,1)S(1)} %encode.2.refs_0_, bf16[896,2048]{1,0:T(8,128)(2,1)S(1)} %copy-done.1), kind=kOutput, calls=%fused_computation.7 | convolution fusion | flops 1410072576 | bytes 5931008 | tf_op jit(solution)/shard_map/dot_general | solution.py:195
  79.4 1.1 %encode.3.refs_0_.refs_1_ = bf16[384,896]{1,0:T(8,128)(2,1)S(1)} custom-call(bf16[384,896]{1,0:T(8,128)(2,1)S(1)} %collective-permute-done.5.raw_ref, bf16[896,896]{1,0:T(8,128)(2,1)S(1)} %bitcast.52), custom_call_target="tpu_custom_call" | custom-call | flops 616562688 | bytes 2981888 | tf_op jit(solution)/shard_map/encode/pallas_call | solution.py:45
  80.6 0.7 copy-done.3
  81.3 8.9 %attend_own.1.refs_11_ = bf16[352,4096]{1,0:T(8,128)(2,1)} custom-call(s32[2]{0:T(128)S(1)} %pad_add_fusion.info_ref, bf16[384,896]{1,0:T(8,128)(2,1)S(1)} %encode.3.refs_0_.refs_1_, bf16[384,2048]{1,0:T(8,128)(2,1)S(1)} %convolution_convert_fusion.refs_1_, bf16[384,2048]{1,0:T(8,128)(2,1)S(1)} %convolution_convert_fusion.1.refs_2_, ...), custom_call_target="tpu_custom_call" | custom-call | flops 3187671040 | bytes 10911744 | tf_op jit(solution)/shard_map/attend_own/pallas_call | solution.py:151
  90.2 14.1 %attend_sent.1 = bf16[352,4096]{1,0:T(8,128)(2,1)} custom-call(s32[5]{0:T(128)S(1)} %stack.45.info_ref, bf16[384,896]{1,0:T(8,128)(2,1)S(1)} %encode.2.refs_0_, bf16[384,896]{1,0:T(8,128)(2,1)S(1)} %encode.3.refs_0_.refs_1_, bf16[896,512]{1,0:T(8,128)(2,1)} %collective-permute-done.6.refs_2_, ...), custom_call_target="tpu_custom_call", output_to_operand_aliasing={{}: (12, {})} | custom-call | flops 6006243328 | bytes 11599872 | tf_op jit(solution)/shard_map/attend_sent/pallas_call | solution.py:174
  (51 shorter events, 0.7 us)
Async XLA Ops:
  0.0 9.1 %copy-start = (bf16[8,32,896]{2,1,0:T(8,128)(2,1)S(1)}, bf16[8,32,896]{2,1,0:T(8,128)(2,1)}, u32[]{:S(2)}) copy-start(bf16[8,32,896]{2,1,0:T(8,128)(2,1)} %param.8) | copy-start | bytes 1376260
  0.0 11.1 %collective-permute-start.2 = (bf16[56,896]{1,0:T(8,128)(2,1)}, bf16[56,896]{1,0:T(8,128)(2,1)S(1)}, u32[]{:S(2)}, u32[]{:S(2)}) collective-permute-start(bf16[56,896]{1,0:T(8,128)(2,1)} %param.9), channel_id=1, source_target_pairs={{0,24},{2,26},{4,28},{6,30},{8,16},{10,18},{12,20},{14,22},{16,8},... | collective-permute-start | bytes 301064 | tf_op jit(solution)/shard_map/ppermute | solution.py:23
  3.3 8.2 %collective-permute-start = (bf16[56,896]{1,0:T(8,128)(2,1)}, bf16[56,896]{1,0:T(8,128)(2,1)S(1)}, u32[]{:S(2)}, u32[]{:S(2)}) collective-permute-start(bf16[56,896]{1,0:T(8,128)(2,1)} %param.9), channel_id=1, source_target_pairs={{0,16},{2,18},{4,20},{6,22},{8,24},{10,26},{12,28},{14,30},{16,0},... | collective-permute-start | bytes 301064 | tf_op jit(solution)/shard_map/ppermute | solution.py:23
  3.3 8.2 %collective-permute-start.1 = (bf16[56,896]{1,0:T(8,128)(2,1)}, bf16[56,896]{1,0:T(8,128)(2,1)S(1)}, u32[]{:S(2)}, u32[]{:S(2)}) collective-permute-start(bf16[56,896]{1,0:T(8,128)(2,1)} %param.9), channel_id=1, source_target_pairs={{0,8},{2,10},{4,12},{6,14},{8,0},{10,2},{12,4},{14,6},{16,24},{18,... | collective-permute-start | bytes 301064 | tf_op jit(solution)/shard_map/ppermute | solution.py:23
  3.7 4.1 %copy-start.6 = (s32[176,2]{0,1:T(2,128)S(1)}, s32[176,2]{0,1:T(2,128)}, u32[]{:S(2)}) copy-start(s32[176,2]{0,1:T(2,128)} %param.12) | copy-start | bytes 4228
  4.9 42.7 %collective-permute-start.10 = (bf16[896,512]{1,0:T(8,128)(2,1)S(1)}, bf16[896,512]{1,0:T(8,128)(2,1)}, u32[]{:S(2)}, u32[]{:S(2)}) collective-permute-start(bf16[896,512]{1,0:T(8,128)(2,1)S(1)} %constant_dynamic-slice_fusion), channel_id=1, source_target_pairs={{0,1},{1,0},{2,3},{3,2},{4,5},{5,4},{6,7},{7,6},{8,9},{9,8},{10,11... | collective-permute-start | bytes 2752520 | tf_op jit(solution)/shard_map/ppermute | solution.py:28
  7.5 40.7 %collective-permute-start.6 = (bf16[896,512]{1,0:T(8,128)(2,1)S(1)}, bf16[896,512]{1,0:T(8,128)(2,1)}, u32[]{:S(2)}, u32[]{:S(2)}) collective-permute-start(bf16[896,512]{1,0:T(8,128)(2,1)S(1)} %constant_dynamic-slice_fusion.1), channel_id=1, source_target_pairs={{0,1},{1,0},{2,3},{3,2},{4,5},{5,4},{6,7},{7,6},{8,9},{9,8},{10,11... | collective-permute-start | bytes 2752520 | tf_op jit(solution)/shard_map/ppermute | solution.py:28
  9.1 2.5 %copy-start.5 = (bf16[56,896]{1,0:T(8,128)(2,1)S(1)}, bf16[56,896]{1,0:T(8,128)(2,1)}, u32[]{:S(2)}) copy-start(bf16[56,896]{1,0:T(8,128)(2,1)} %param.9) | copy-start | bytes 301060
  11.6 46.0 %all-to-all-start = ((bf16[16,2,32,896]{3,2,1,0:T(8,128)(2,1)}), bf16[16,2,32,896]{3,2,1,0:T(8,128)(2,1)}, u32[]{:S(2)}, u32[]{:S(2)}) async-start(bf16[16,2,32,896]{3,2,1,0:T(8,128)(2,1)} %bitcast.6), calls=%async_computation | async-start | bytes 3670016 | tf_op jit(solution)/shard_map/all_to_all | solution.py:229
  20.2 26.8 %copy-start.4 = (s32[16]{0:T(128)S(1)}, s32[16]{0:T(128)}, u32[]{:S(2)}) copy-start(s32[16]{0:T(128)} %constant.119.clone) | copy-start | bytes 196
  20.9 23.3 %collective-permute-start.3 = (bf16[4,56,896]{2,1,0:T(8,128)(2,1)S(1)}, bf16[4,56,896]{2,1,0:T(8,128)(2,1)S(1)}, u32[]{:S(2)}, u32[]{:S(2)}) collective-permute-start(bf16[4,56,896]{2,1,0:T(8,128)(2,1)S(1)} %pad_maximum_fusion), channel_id=1, source_target_pairs={{0,4},{2,6},{4,0},{6,2},{8,12},{10,14},{12,8},{14,10},{16,20},{18,... | collective-permute-start | bytes 1204232 | tf_op jit(solution)/shard_map/ppermute | solution.py:23
  45.2 4.0 %collective-permute-start.4 = (bf16[8,56,896]{2,1,0:T(8,128)(2,1)}, bf16[8,56,896]{2,1,0:T(8,128)(2,1)S(1)}, u32[]{:S(2)}, u32[]{:S(2)}) collective-permute-start(bf16[8,56,896]{2,1,0:T(8,128)(2,1)} %get-tuple-element.13), channel_id=1, source_target_pairs={{0,2},{2,0},{4,6},{6,4},{8,10},{10,8},{12,14},{14,12},{16,18},{18,... | collective-permute-start | bytes 2408456 | tf_op jit(solution)/shard_map/ppermute | solution.py:23
  47.6 25.5 %collective-permute-start.11 = (bf16[896,512]{1,0:T(8,128)(2,1)}, bf16[896,512]{1,0:T(8,128)(2,1)}, u32[]{:S(2)}, u32[]{:S(2)}) collective-permute-start(bf16[896,512]{1,0:T(8,128)(2,1)} %collective-permute-done.10.refs_6_), channel_id=1, source_target_pairs={{0,4},{2,6},{4,0},{6,2},{8,12},{10,14},{12,8},{14,10},{16,20},{18,... | collective-permute-start | bytes 2752520 | tf_op jit(solution)/shard_map/ppermute | solution.py:23
  48.2 28.8 %collective-permute-start.7 = (bf16[896,512]{1,0:T(8,128)(2,1)}, bf16[896,512]{1,0:T(8,128)(2,1)}, u32[]{:S(2)}, u32[]{:S(2)}) collective-permute-start(bf16[896,512]{1,0:T(8,128)(2,1)} %collective-permute-done.6.refs_2_), channel_id=1, source_target_pairs={{0,8},{2,10},{4,12},{6,14},{8,0},{10,2},{12,4},{14,6},{16,24},{18,... | collective-permute-start | bytes 2752520 | tf_op jit(solution)/shard_map/ppermute | solution.py:23
  48.4 41.8 %collective-permute-start.12 = (bf16[896,512]{1,0:T(8,128)(2,1)}, bf16[896,512]{1,0:T(8,128)(2,1)}, u32[]{:S(2)}, u32[]{:S(2)}) collective-permute-start(bf16[896,512]{1,0:T(8,128)(2,1)} %collective-permute-done.10.refs_6_), channel_id=1, source_target_pairs={{0,2},{2,0},{4,6},{6,4},{8,10},{10,8},{12,14},{14,12},{16,18},{18,... | collective-permute-start | bytes 2752520 | tf_op jit(solution)/shard_map/ppermute | solution.py:23
  49.1 41.0 %collective-permute-start.8 = (bf16[896,512]{1,0:T(8,128)(2,1)}, bf16[896,512]{1,0:T(8,128)(2,1)}, u32[]{:S(2)}, u32[]{:S(2)}) collective-permute-start(bf16[896,512]{1,0:T(8,128)(2,1)} %collective-permute-done.6.refs_2_), channel_id=1, source_target_pairs={{0,2},{2,0},{4,6},{6,4},{8,10},{10,8},{12,14},{14,12},{16,18},{18,... | collective-permute-start | bytes 2752520 | tf_op jit(solution)/shard_map/ppermute | solution.py:23
  60.7 18.7 %collective-permute-start.5 = (bf16[384,896]{1,0:T(8,128)(2,1)}, bf16[384,896]{1,0:T(8,128)(2,1)S(1)}, u32[]{:S(2)}, u32[]{:S(2)}) collective-permute-start(bf16[384,896]{1,0:T(8,128)(2,1)} %bitcast.24), channel_id=1, source_target_pairs={{0,1},{1,0},{2,3},{3,2},{4,5},{5,4},{6,7},{7,6},{8,9},{9,8},{10,11... | collective-permute-start | bytes 2064392 | tf_op jit(solution)/shard_map/ppermute | solution.py:28
  65.2 12.4 %copy-start.1 = (bf16[896,2048]{1,0:T(8,128)(2,1)S(1)}, bf16[896,2048]{1,0:T(8,128)(2,1)}, u32[]{:S(2)}) copy-start(bf16[896,2048]{1,0:T(8,128)(2,1)} %refs_3_.1) | copy-start | bytes 11010052
  73.2 17.0 %collective-permute-start.13 = (bf16[896,512]{1,0:T(8,128)(2,1)}, bf16[896,512]{1,0:T(8,128)(2,1)S(1)}, u32[]{:S(2)}, u32[]{:S(2)}) collective-permute-start(bf16[896,512]{1,0:T(8,128)(2,1)} %collective-permute-done.11.refs_7_), channel_id=1, source_target_pairs={{0,2},{2,0},{4,6},{6,4},{8,10},{10,8},{12,14},{14,12},{16,18},{18,... | collective-permute-start | bytes 2752520 | tf_op jit(solution)/shard_map/ppermute | solution.py:23
  77.0 13.1 %collective-permute-start.9 = (bf16[896,512]{1,0:T(8,128)(2,1)}, bf16[896,512]{1,0:T(8,128)(2,1)S(1)}, u32[]{:S(2)}, u32[]{:S(2)}) collective-permute-start(bf16[896,512]{1,0:T(8,128)(2,1)} %collective-permute-done.7.refs_3_), channel_id=1, source_target_pairs={{0,2},{2,0},{4,6},{6,4},{8,10},{10,8},{12,14},{14,12},{16,18},{18,... | collective-permute-start | bytes 2752520 | tf_op jit(solution)/shard_map/ppermute | solution.py:23
  77.6 3.0 %copy-start.2 = (bf16[896,2048]{1,0:T(8,128)(2,1)S(1)}, bf16[896,2048]{1,0:T(8,128)(2,1)}, u32[]{:S(2)}) copy-start(bf16[896,2048]{1,0:T(8,128)(2,1)} %refs_4_.1) | copy-start | bytes 11010052
  79.4 1.9 %copy-start.3 = (bf16[352,4096]{1,0:T(8,128)(2,1)S(1)}, bf16[352,4096]{1,0:T(8,128)(2,1)}, u32[]{:S(2)}) copy-start(bf16[352,4096]{1,0:T(8,128)(2,1)} %refs_10_.1) | copy-start | bytes 8650756

commit v5 on v3

--- a/solution.py
+++ b/solution.py
@@ -53,7 +53,7 @@
     )(raw_rows, w_encoder)
 
 
-def attend_heads(keys_of, values_of, q_ref, o_ref, qf_ref, of_ref, offset):
+def attend_heads(keys_of, make_values, q_ref, o_ref, qf_ref, of_ref, offset):
     rows, wide = q_ref.shape
     spans = qf_ref.shape[0] // SPAN
     qf_ref[pl.ds(offset, rows), :] = q_ref[...]
@@ -65,6 +65,7 @@
         )
         for lines, span, cols in places
     ]
+    values_of = make_values()
     probs = []
     for score in scores:
         highest = jnp.max(score, axis=-1, keepdims=True)
@@ -93,9 +94,13 @@
     wide = q_ref.shape[1]
     here = pl.ds(pl.multiple_of(pl.program_id(0) * wide, wide), wide)
     k_refs = [first_k.at[:, here], *make_parts(enc_refs, wk_ref[:, here], ks_ref)]
-    v_refs = [first_v.at[:, here], *make_parts(enc_refs, wv_ref[:, here], vs_ref)]
+
+    def make_values():
+        v_refs = [first_v.at[:, here], *make_parts(enc_refs, wv_ref[:, here], vs_ref)]
+        return functools.partial(span_rows, v_refs)
+
     attend_heads(
-        functools.partial(span_rows, k_refs), functools.partial(span_rows, v_refs),
+        functools.partial(span_rows, k_refs), make_values,
         q_ref, o_ref, qf_ref, of_ref, pl.multiple_of(info_ref[0], 16),
     )
 
@@ -117,12 +122,16 @@
         def _(piece=piece):
             for copy in fetch(piece, piece % 2):
                 copy.start()
-    for copy in fetch(0, slot):
-        copy.wait()
+    keys_here, values_here = fetch(0, slot)
+    keys_here.wait()
     k_refs = make_parts(enc_refs, w_ref[slot, 0], ks_ref)
-    v_refs = make_parts(enc_refs, w_ref[slot, 1], vs_ref)
+
+    def make_values():
+        values_here.wait()
+        return functools.partial(span_rows, make_parts(enc_refs, w_ref[slot, 1], vs_ref))
+
     attend_heads(
-        functools.partial(span_rows, k_refs), functools.partial(span_rows, v_refs),
+        functools.partial(span_rows, k_refs), make_values,
         q_ref, o_ref, qf_ref, of_ref, pl.multiple_of(info_ref[0], 16),
     )
 

time: 106 us -> 106 us (level)
  no operation moved by 1% of the time
where the time goes in v5:
time: 106 us; the launch traced here: 104 us
  waiting for transfers between devices  34.9 us (33%)
  Pallas kernels  25.4 us (24%)
  local copies, waits for them, and re-layouts  20.1 us (19%)
  starting transfers between devices  17 us (16%)
  matrix products  5.77 us (5%)
    ppermute x11, waiting for transfers between devices, xor_permute(): return lax.ppermute(x, 'seq', [(i, i ^ bits) for i in range(count)])  29.4 us
    pallas_call x1, Pallas kernels, attend_sent(): pl.pallas_call(functools.partial(sent_kernel, parts), grid_spec=pltpu.Pre...  14.3 us
    pallas_call x1, Pallas kernels, attend_own(): pl.pallas_call(functools.partial(own_kernel, len(encoded) + 1), grid_spec...  8.82 us
    all_to_all x1, starting transfers between devices, per_device(): lax.all_to_all(entries, 'seq', split_axis=0, concat_axis=0, tiled=True)  7.52 us
    ppermute x11, starting transfers between devices, xor_permute(): return lax.ppermute(x, 'seq', [(i, i ^ bits) for i in range(count)])  6.62 us
    gather x4, local copies, waits for them, and re-layouts, neighbours_of(): return flat_arrived[cited_slot[places]].reshape(-1, flat_arrived.shape[2])  6.46 us
    dot_general x2, matrix products, project(): jnp.dot(rows, weights, preferred_element_type=jnp.float32)  5.77 us
    all_to_all x1, waiting for transfers between devices, per_device(): lax.all_to_all(entries, 'seq', split_axis=0, concat_axis=0, tiled=True)  5.45 us
  transfers between devices with their start and end apart: 15, of which 4 were waited for; matrix products, arithmetic and copies ran while one was open for 25% of the time, Pallas kernels for 11%

profile of v5, /device:TPU:3, one launch (start us, length us, event | category | flops | bytes accessed | tf_op | source)
XLA Modules:
  0.0 104.4 jit_solution(12849441926511121016)
XLA Ops:
  0.0 3.3 %collective-permute-start.2 = (bf16[56,896]{1,0:T(8,128)(2,1)}, bf16[56,896]{1,0:T(8,128)(2,1)S(1)}, u32[]{:S(2)}, u32[]{:S(2)}) collective-permute-start(bf16[56,896]{1,0:T(8,128)(2,1)} %param.9), channel_id=1, source_target_pairs={{0,24},{2,26},{4,28},{6,30},{8,16},{10,18},{12,20},{14,22},{16,8},... | collective-permute-start | bytes 301064 | tf_op jit(solution)/shard_map/ppermute | solution.py:23
  3.3 0.4 collective-permute-start.1
  3.7 1.3 %constant_dynamic-slice_fusion = bf16[896,512]{1,0:T(8,128)(2,1)S(1)} fusion(bf16[896,2048]{1,0:T(8,128)(2,1)} %refs_4_.1, s32[]{:T(128)S(6)} %select_n.156), kind=kLoop, calls=%fused_computation.51 | loop fusion | bytes 1835012 | tf_op jit(solution)/shard_map/dynamic_slice | solution.py:264
  4.9 1.3 %collective-permute-start.10 = (bf16[896,512]{1,0:T(8,128)(2,1)S(1)}, bf16[896,512]{1,0:T(8,128)(2,1)}, u32[]{:S(2)}, u32[]{:S(2)}) collective-permute-start(bf16[896,512]{1,0:T(8,128)(2,1)S(1)} %constant_dynamic-slice_fusion), channel_id=1, source_target_pairs={{0,1},{1,0},{2,3},{3,2},{4,5},{5,4},{6,7},{7,6},{8,9},{9,8},{10,11... | collective-permute-start | bytes 2752520 | tf_op jit(solution)/shard_map/ppermute | solution.py:28
  6.2 1.2 %constant_dynamic-slice_fusion.1 = bf16[896,512]{1,0:T(8,128)(2,1)S(1)} fusion(bf16[896,2048]{1,0:T(8,128)(2,1)} %refs_3_.1, s32[]{:T(128)S(6)} %select_n.156), kind=kLoop, calls=%fused_computation.52 | loop fusion | bytes 1835012 | tf_op jit(solution)/shard_map/dynamic_slice | solution.py:264
  7.5 0.3 collective-permute-start.6
  7.8 0.1 copy.32
  7.9 0.1 reshape.260
  8.1 0.1 copy.33
  8.1 0.5 convert_reduce_fusion
  8.8 0.1 select_reduce_fusion
  8.9 0.1 copy.35
  9.0 0.1 reshape.267
  9.1 2.0 %gather_fusion = bf16[32,32,896]{2,1,0:T(8,128)(2,1)} fusion(bf16[8,32,896]{2,1,0:T(8,128)(2,1)S(1)} %copy-done, s32[1024]{0:T(1024)S(1)} %pad_clamp_fusion.6), kind=kCustom, calls=%fused_computation | custom fusion | bytes 3670144 | tf_op jit(solution)/shard_map/gather | solution.py:237
  11.1 0.5 collective-permute-done
  11.6 7.5 %all-to-all-start = ((bf16[16,2,32,896]{3,2,1,0:T(8,128)(2,1)}), bf16[16,2,32,896]{3,2,1,0:T(8,128)(2,1)}, u32[]{:S(2)}, u32[]{:S(2)}) async-start(bf16[16,2,32,896]{3,2,1,0:T(8,128)(2,1)} %bitcast.6), calls=%async_computation | async-start | bytes 3670016 | tf_op jit(solution)/shard_map/all_to_all | solution.py:238
  19.2 0.1 add.242
  19.4 0.1 add.230
  19.5 0.7 gather_fusion.5
  20.2 0.7 constant_dynamic-update-slice_fusion.4
  20.9 0.1 collective-permute-start.3
  21.0 0.7 constant_dynamic-update-slice_fusion.3
  21.7 0.7 constant_dynamic-update-slice_fusion.2
  22.4 0.7 constant_dynamic-update-slice_fusion.1
  23.1 21.1 %collective-permute-done.3 = bf16[4,56,896]{2,1,0:T(8,128)(2,1)S(1)} collective-permute-done((bf16[4,56,896]{2,1,0:T(8,128)(2,1)S(1)}, bf16[4,56,896]{2,1,0:T(8,128)(2,1)S(1)}, u32[]{:S(2)}, u32[]{:S(2)}) %collective-permute-start.3) | collective-permute-done | bytes 401440 | tf_op jit(solution)/shard_map/ppermute | solution.py:23
  44.2 1.0 constant_dynamic-update-slice_fusion
  45.2 1.1 %collective-permute-start.4 = (bf16[8,56,896]{2,1,0:T(8,128)(2,1)}, bf16[8,56,896]{2,1,0:T(8,128)(2,1)S(1)}, u32[]{:S(2)}, u32[]{:S(2)}) collective-permute-start(bf16[8,56,896]{2,1,0:T(8,128)(2,1)} %get-tuple-element.13), channel_id=1, source_target_pairs={{0,2},{2,0},{4,6},{6,4},{8,10},{10,8},{12,14},{14,12},{16,18},{18,... | collective-permute-start | bytes 2408456 | tf_op jit(solution)/shard_map/ppermute | solution.py:23
  46.3 0.7 gather_fusion.1
  47.0 0.7 gather_fusion.3
  47.7 0.6 collective-permute-start.7
  48.3 0.1 stack.45.info_ref
  48.4 0.4 collective-permute-start.12
  48.8 0.2 collective-permute-start.8
  49.0 1.0 constant_dynamic-update-slice_fusion.5
  50.0 2.2 %gather_fusion.4 = bf16[16,56,896]{2,1,0:T(8,128)(2,1)S(1)} fusion(bf16[16,56,896]{2,1,0:T(8,128)(2,1)} %constant_dynamic-update-slice_fusion.5, s32[1024]{0:T(1024)S(1)} %pad_clamp_fusion.2), kind=kCustom, calls=%fused_computation.4 | custom fusion | bytes 3211328 | tf_op jit(solution)/shard_map/gather | solution.py:222
  52.2 5.4 %all-to-all-done = bf16[16,2,32,896]{3,2,1,0:T(8,128)(2,1)} async-done(((bf16[16,2,32,896]{3,2,1,0:T(8,128)(2,1)}), bf16[16,2,32,896]{3,2,1,0:T(8,128)(2,1)}, u32[]{:S(2)}, u32[]{:S(2)}) %all-to-all-start) | async-done | bytes 1835040 | tf_op jit(solution)/shard_map/all_to_all | solution.py:238
  57.7 3.0 %gather_fusion.6 = bf16[12,32,896]{2,1,0:T(8,128)(2,1)} fusion(bf16[32,32,896]{2,1,0:T(8,128)(2,1)} %bitcast.11, s32[1024]{0:T(1024)S(1)} %pad_clamp_fusion), kind=kCustom, calls=%fused_computation.6 | custom fusion | bytes 1376304 | tf_op jit(solution)/shard_map/gather | solution.py:249
  60.7 1.2 %collective-permute-start.5 = (bf16[384,896]{1,0:T(8,128)(2,1)}, bf16[384,896]{1,0:T(8,128)(2,1)S(1)}, u32[]{:S(2)}, u32[]{:S(2)}) collective-permute-start(bf16[384,896]{1,0:T(8,128)(2,1)} %bitcast.24), channel_id=1, source_target_pairs={{0,1},{1,0},{2,3},{3,2},{4,5},{5,4},{6,7},{7,6},{8,9},{9,8},{10,11... | collective-permute-start | bytes 2064392 | tf_op jit(solution)/shard_map/ppermute | solution.py:28
  61.9 2.2 %gather_fusion.2 = bf16[12,32,896]{2,1,0:T(8,128)(2,1)S(1)} fusion(bf16[32,32,896]{2,1,0:T(8,128)(2,1)} %bitcast.11, s32[1024]{0:T(1024)S(1)} %pad_clamp_fusion.4), kind=kCustom, calls=%fused_computation.2 | custom fusion | bytes 1376304 | tf_op jit(solution)/shard_map/gather | solution.py:249
  64.1 1.1 %encode.2.refs_0_ = bf16[384,896]{1,0:T(8,128)(2,1)S(1)} custom-call(bf16[384,896]{1,0:T(8,128)(2,1)S(1)} %bitcast.53, bf16[896,896]{1,0:T(8,128)(2,1)S(1)} %bitcast.51), custom_call_target="tpu_custom_call" | custom-call | flops 616562688 | bytes 2981888 | tf_op jit(solution)/shard_map/encode/pallas_call | solution.py:45
  65.2 4.0 %convolution_convert_fusion.1.refs_2_ = bf16[384,2048]{1,0:T(8,128)(2,1)S(1)} fusion(bf16[384,896]{1,0:T(8,128)(2,1)S(1)} %encode.2.refs_0_, bf16[896,2048]{1,0:T(8,128)(2,1)} %refs_4_.1), kind=kOutput, calls=%fused_computation.8 | convolution fusion | flops 1410072576 | bytes 5931008 | tf_op jit(solution)/shard_map/dot_general | solution.py:204
  69.2 7.8 %collective-permute-done.11.refs_7_ = bf16[896,512]{1,0:T(8,128)(2,1)} collective-permute-done((bf16[896,512]{1,0:T(8,128)(2,1)}, bf16[896,512]{1,0:T(8,128)(2,1)}, u32[]{:S(2)}, u32[]{:S(2)}) %collective-permute-start.11) | collective-permute-done | bytes 917536 | tf_op jit(solution)/shard_map/ppermute | solution.py:23
  77.1 0.4 collective-permute-start.13
  77.7 1.8 %convolution_convert_fusion.refs_1_ = bf16[384,2048]{1,0:T(8,128)(2,1)S(1)} fusion(bf16[384,896]{1,0:T(8,128)(2,1)S(1)} %encode.2.refs_0_, bf16[896,2048]{1,0:T(8,128)(2,1)S(1)} %copy-done.1), kind=kOutput, calls=%fused_computation.7 | convolution fusion | flops 1410072576 | bytes 5931008 | tf_op jit(solution)/shard_map/dot_general | solution.py:204
  79.5 1.1 %encode.3.refs_0_.refs_1_ = bf16[384,896]{1,0:T(8,128)(2,1)S(1)} custom-call(bf16[384,896]{1,0:T(8,128)(2,1)S(1)} %collective-permute-done.5.raw_ref, bf16[896,896]{1,0:T(8,128)(2,1)S(1)} %bitcast.52), custom_call_target="tpu_custom_call" | custom-call | flops 616562688 | bytes 2981888 | tf_op jit(solution)/shard_map/encode/pallas_call | solution.py:45
  80.6 0.7 copy-done.3
  81.3 8.8 %attend_own.1.refs_11_ = bf16[352,4096]{1,0:T(8,128)(2,1)} custom-call(s32[2]{0:T(128)S(1)} %pad_add_fusion.info_ref, bf16[384,896]{1,0:T(8,128)(2,1)S(1)} %encode.3.refs_0_.refs_1_, bf16[384,2048]{1,0:T(8,128)(2,1)S(1)} %convolution_convert_fusion.refs_1_, bf16[384,2048]{1,0:T(8,128)(2,1)S(1)} %convolution_convert_fusion.1.refs_2_, ...), custom_call_target="tpu_custom_call" | custom-call | flops 3187671040 | bytes 10911744 | tf_op jit(solution)/shard_map/attend_own/pallas_call | solution.py:160
  90.2 14.3 %attend_sent.1 = bf16[352,4096]{1,0:T(8,128)(2,1)} custom-call(s32[5]{0:T(128)S(1)} %stack.45.info_ref, bf16[384,896]{1,0:T(8,128)(2,1)S(1)} %encode.2.refs_0_, bf16[384,896]{1,0:T(8,128)(2,1)S(1)} %encode.3.refs_0_.refs_1_, bf16[896,512]{1,0:T(8,128)(2,1)} %collective-permute-done.6.refs_2_, ...), custom_call_target="tpu_custom_call", output_to_operand_aliasing={{}: (12, {})} | custom-call | flops 6006243328 | bytes 11599872 | tf_op jit(solution)/shard_map/attend_sent/pallas_call | solution.py:183
  (51 shorter events, 0.7 us)
Async XLA Ops:
  0.0 9.1 %copy-start = (bf16[8,32,896]{2,1,0:T(8,128)(2,1)S(1)}, bf16[8,32,896]{2,1,0:T(8,128)(2,1)}, u32[]{:S(2)}) copy-start(bf16[8,32,896]{2,1,0:T(8,128)(2,1)} %param.8) | copy-start | bytes 1376260
  0.0 11.1 %collective-permute-start.2 = (bf16[56,896]{1,0:T(8,128)(2,1)}, bf16[56,896]{1,0:T(8,128)(2,1)S(1)}, u32[]{:S(2)}, u32[]{:S(2)}) collective-permute-start(bf16[56,896]{1,0:T(8,128)(2,1)} %param.9), channel_id=1, source_target_pairs={{0,24},{2,26},{4,28},{6,30},{8,16},{10,18},{12,20},{14,22},{16,8},... | collective-permute-start | bytes 301064 | tf_op jit(solution)/shard_map/ppermute | solution.py:23
  3.3 8.2 %collective-permute-start = (bf16[56,896]{1,0:T(8,128)(2,1)}, bf16[56,896]{1,0:T(8,128)(2,1)S(1)}, u32[]{:S(2)}, u32[]{:S(2)}) collective-permute-start(bf16[56,896]{1,0:T(8,128)(2,1)} %param.9), channel_id=1, source_target_pairs={{0,16},{2,18},{4,20},{6,22},{8,24},{10,26},{12,28},{14,30},{16,0},... | collective-permute-start | bytes 301064 | tf_op jit(solution)/shard_map/ppermute | solution.py:23
  3.3 8.2 %collective-permute-start.1 = (bf16[56,896]{1,0:T(8,128)(2,1)}, bf16[56,896]{1,0:T(8,128)(2,1)S(1)}, u32[]{:S(2)}, u32[]{:S(2)}) collective-permute-start(bf16[56,896]{1,0:T(8,128)(2,1)} %param.9), channel_id=1, source_target_pairs={{0,8},{2,10},{4,12},{6,14},{8,0},{10,2},{12,4},{14,6},{16,24},{18,... | collective-permute-start | bytes 301064 | tf_op jit(solution)/shard_map/ppermute | solution.py:23
  3.7 4.1 %copy-start.6 = (s32[176,2]{0,1:T(2,128)S(1)}, s32[176,2]{0,1:T(2,128)}, u32[]{:S(2)}) copy-start(s32[176,2]{0,1:T(2,128)} %param.12) | copy-start | bytes 4228
  4.9 42.7 %collective-permute-start.10 = (bf16[896,512]{1,0:T(8,128)(2,1)S(1)}, bf16[896,512]{1,0:T(8,128)(2,1)}, u32[]{:S(2)}, u32[]{:S(2)}) collective-permute-start(bf16[896,512]{1,0:T(8,128)(2,1)S(1)} %constant_dynamic-slice_fusion), channel_id=1, source_target_pairs={{0,1},{1,0},{2,3},{3,2},{4,5},{5,4},{6,7},{7,6},{8,9},{9,8},{10,11... | collective-permute-start | bytes 2752520 | tf_op jit(solution)/shard_map/ppermute | solution.py:28
  7.5 40.2 %collective-permute-start.6 = (bf16[896,512]{1,0:T(8,128)(2,1)S(1)}, bf16[896,512]{1,0:T(8,128)(2,1)}, u32[]{:S(2)}, u32[]{:S(2)}) collective-permute-start(bf16[896,512]{1,0:T(8,128)(2,1)S(1)} %constant_dynamic-slice_fusion.1), channel_id=1, source_target_pairs={{0,1},{1,0},{2,3},{3,2},{4,5},{5,4},{6,7},{7,6},{8,9},{9,8},{10,11... | collective-permute-start | bytes 2752520 | tf_op jit(solution)/shard_map/ppermute | solution.py:28
  9.1 2.5 %copy-start.5 = (bf16[56,896]{1,0:T(8,128)(2,1)S(1)}, bf16[56,896]{1,0:T(8,128)(2,1)}, u32[]{:S(2)}) copy-start(bf16[56,896]{1,0:T(8,128)(2,1)} %param.9) | copy-start | bytes 301060
  11.6 46.0 %all-to-all-start = ((bf16[16,2,32,896]{3,2,1,0:T(8,128)(2,1)}), bf16[16,2,32,896]{3,2,1,0:T(8,128)(2,1)}, u32[]{:S(2)}, u32[]{:S(2)}) async-start(bf16[16,2,32,896]{3,2,1,0:T(8,128)(2,1)} %bitcast.6), calls=%async_computation | async-start | bytes 3670016 | tf_op jit(solution)/shard_map/all_to_all | solution.py:238
  20.2 26.8 %copy-start.4 = (s32[16]{0:T(128)S(1)}, s32[16]{0:T(128)}, u32[]{:S(2)}) copy-start(s32[16]{0:T(128)} %constant.119.clone) | copy-start | bytes 196
  20.9 23.3 %collective-permute-start.3 = (bf16[4,56,896]{2,1,0:T(8,128)(2,1)S(1)}, bf16[4,56,896]{2,1,0:T(8,128)(2,1)S(1)}, u32[]{:S(2)}, u32[]{:S(2)}) collective-permute-start(bf16[4,56,896]{2,1,0:T(8,128)(2,1)S(1)} %pad_maximum_fusion), channel_id=1, source_target_pairs={{0,4},{2,6},{4,0},{6,2},{8,12},{10,14},{12,8},{14,10},{16,20},{18,... | collective-permute-start | bytes 1204232 | tf_op jit(solution)/shard_map/ppermute | solution.py:23
  45.2 3.8 %collective-permute-start.4 = (bf16[8,56,896]{2,1,0:T(8,128)(2,1)}, bf16[8,56,896]{2,1,0:T(8,128)(2,1)S(1)}, u32[]{:S(2)}, u32[]{:S(2)}) collective-permute-start(bf16[8,56,896]{2,1,0:T(8,128)(2,1)} %get-tuple-element.13), channel_id=1, source_target_pairs={{0,2},{2,0},{4,6},{6,4},{8,10},{10,8},{12,14},{14,12},{16,18},{18,... | collective-permute-start | bytes 2408456 | tf_op jit(solution)/shard_map/ppermute | solution.py:23
  47.6 29.4 %collective-permute-start.11 = (bf16[896,512]{1,0:T(8,128)(2,1)}, bf16[896,512]{1,0:T(8,128)(2,1)}, u32[]{:S(2)}, u32[]{:S(2)}) collective-permute-start(bf16[896,512]{1,0:T(8,128)(2,1)} %collective-permute-done.10.refs_6_), channel_id=1, source_target_pairs={{0,8},{2,10},{4,12},{6,14},{8,0},{10,2},{12,4},{14,6},{16,24},{18,... | collective-permute-start | bytes 2752520 | tf_op jit(solution)/shard_map/ppermute | solution.py:23
  47.7 29.8 %collective-permute-start.7 = (bf16[896,512]{1,0:T(8,128)(2,1)}, bf16[896,512]{1,0:T(8,128)(2,1)}, u32[]{:S(2)}, u32[]{:S(2)}) collective-permute-start(bf16[896,512]{1,0:T(8,128)(2,1)} %collective-permute-done.6.refs_2_), channel_id=1, source_target_pairs={{0,4},{2,6},{4,0},{6,2},{8,12},{10,14},{12,8},{14,10},{16,20},{18,... | collective-permute-start | bytes 2752520 | tf_op jit(solution)/shard_map/ppermute | solution.py:23
  48.4 41.7 %collective-permute-start.12 = (bf16[896,512]{1,0:T(8,128)(2,1)}, bf16[896,512]{1,0:T(8,128)(2,1)}, u32[]{:S(2)}, u32[]{:S(2)}) collective-permute-start(bf16[896,512]{1,0:T(8,128)(2,1)} %collective-permute-done.10.refs_6_), channel_id=1, source_target_pairs={{0,2},{2,0},{4,6},{6,4},{8,10},{10,8},{12,14},{14,12},{16,18},{18,... | collective-permute-start | bytes 2752520 | tf_op jit(solution)/shard_map/ppermute | solution.py:23
  48.8 41.4 %collective-permute-start.8 = (bf16[896,512]{1,0:T(8,128)(2,1)}, bf16[896,512]{1,0:T(8,128)(2,1)}, u32[]{:S(2)}, u32[]{:S(2)}) collective-permute-start(bf16[896,512]{1,0:T(8,128)(2,1)} %collective-permute-done.6.refs_2_), channel_id=1, source_target_pairs={{0,2},{2,0},{4,6},{6,4},{8,10},{10,8},{12,14},{14,12},{16,18},{18,... | collective-permute-start | bytes 2752520 | tf_op jit(solution)/shard_map/ppermute | solution.py:23
  60.7 18.8 %collective-permute-start.5 = (bf16[384,896]{1,0:T(8,128)(2,1)}, bf16[384,896]{1,0:T(8,128)(2,1)S(1)}, u32[]{:S(2)}, u32[]{:S(2)}) collective-permute-start(bf16[384,896]{1,0:T(8,128)(2,1)} %bitcast.24), channel_id=1, source_target_pairs={{0,1},{1,0},{2,3},{3,2},{4,5},{5,4},{6,7},{7,6},{8,9},{9,8},{10,11... | collective-permute-start | bytes 2064392 | tf_op jit(solution)/shard_map/ppermute | solution.py:28
  65.2 12.4 %copy-start.1 = (bf16[896,2048]{1,0:T(8,128)(2,1)S(1)}, bf16[896,2048]{1,0:T(8,128)(2,1)}, u32[]{:S(2)}) copy-start(bf16[896,2048]{1,0:T(8,128)(2,1)} %refs_3_.1) | copy-start | bytes 11010052
  77.1 13.1 %collective-permute-start.13 = (bf16[896,512]{1,0:T(8,128)(2,1)}, bf16[896,512]{1,0:T(8,128)(2,1)S(1)}, u32[]{:S(2)}, u32[]{:S(2)}) collective-permute-start(bf16[896,512]{1,0:T(8,128)(2,1)} %collective-permute-done.11.refs_7_), channel_id=1, source_target_pairs={{0,2},{2,0},{4,6},{6,4},{8,10},{10,8},{12,14},{14,12},{16,18},{18,... | collective-permute-start | bytes 2752520 | tf_op jit(solution)/shard_map/ppermute | solution.py:23
  77.5 12.7 %collective-permute-start.9 = (bf16[896,512]{1,0:T(8,128)(2,1)}, bf16[896,512]{1,0:T(8,128)(2,1)S(1)}, u32[]{:S(2)}, u32[]{:S(2)}) collective-permute-start(bf16[896,512]{1,0:T(8,128)(2,1)} %collective-permute-done.7.refs_3_), channel_id=1, source_target_pairs={{0,2},{2,0},{4,6},{6,4},{8,10},{10,8},{12,14},{14,12},{16,18},{18,... | collective-permute-start | bytes 2752520 | tf_op jit(solution)/shard_map/ppermute | solution.py:23
  77.7 3.0 %copy-start.2 = (bf16[896,2048]{1,0:T(8,128)(2,1)S(1)}, bf16[896,2048]{1,0:T(8,128)(2,1)}, u32[]{:S(2)}) copy-start(bf16[896,2048]{1,0:T(8,128)(2,1)} %refs_4_.1) | copy-start | bytes 11010052
  79.5 1.9 %copy-start.3 = (bf16[352,4096]{1,0:T(8,128)(2,1)S(1)}, bf16[352,4096]{1,0:T(8,128)(2,1)}, u32[]{:S(2)}) copy-start(bf16[352,4096]{1,0:T(8,128)(2,1)} %refs_10_.1) | copy-start | bytes 8650756
